TPU v7x, 32 devices: a whole 2x2x4 slice. The times are simulated.
32 devices in a mesh: dev: 32 (over z, y, x, core).
Axes of the slice: x: 2, y: 2, z: 4, core: 2. Of those that a mesh axis runs over, the one named last changes fastest.
Arguments:
- row_table: float32 [1024, 32, 512], P('dev'), may hold values from -3 to 3
- col_table: float32 [1024, 32, 512], P('dev'), may hold values from -3 to 3
- row_accum: float32 [1024, 32, 512], P('dev'), may hold values from 0.05 to 0.5
- col_accum: float32 [1024, 32, 512], P('dev'), may hold values from 0.05 to 0.5
- row_margin: float32 [1024, 32], P('dev'), may hold values from -2 to 1
- col_margin: float32 [1024, 32], P('dev'), may hold values from -2 to 1
- row_blocks: int32 [64], P('dev'), may hold values from 0 to 31
- col_blocks: int32 [64], P('dev'), may hold values from 0 to 31
- slot_of: int32 [32], replicated, may hold values from 0 to 31, each once
- counts: int32 [64, 1024, 1024], P('dev'), may hold values from 0 to 199, as said below
Outputs:
- new_row_table: float32 [1024, 32, 512], P('dev')
- new_col_table: float32 [1024, 32, 512], P('dev')
- new_row_accum: float32 [1024, 32, 512], P('dev')
- new_col_accum: float32 [1024, 32, 512], P('dev')
Inputs may be any that keep to these rules, and one draw needn't show every extreme that they name: `slot_of`: each block appears once. `counts`: about six cells in ten are nonzero.
All inputs are finite; a program needn't handle non-finite values.
Results may differ from a plain program's by a relative error of at most 0.0003.
Values sent between devices are 32-bit elements; how exact they have to be, the bound alone decides.
No kernel may reach another device: no remote copies, remote signals or barrier semaphores. Data moves between devices by JAX's collectives and lax.ppermute only.
A program may use at most 128 MiB of HBM per device.

v0:
```python
import jax
import jax.numpy as jnp
from jax import lax
from jax.sharding import PartitionSpec as P


def shard_grads(rows_block, cols_block, margin_r, margin_c, tile_counts):
    high = lax.Precision.HIGHEST
    logits = jnp.dot(rows_block, cols_block.T, precision=high, preferred_element_type=jnp.float32)
    values = tile_counts.astype(jnp.float32)
    target = jnp.log(jnp.maximum(values, 1.0)) - margin_r[:, None] - margin_c[None, :]
    error = logits - target
    confidence = 0.1 + 0.25 * jnp.sqrt(values)
    scaled = (
        jnp.where(tile_counts > 0, confidence * error, jax.nn.sigmoid(error)) / tile_counts.shape[0]
    )
    row_grad = jnp.dot(scaled, cols_block, precision=high, preferred_element_type=jnp.float32)
    col_grad = lax.dot_general(
        scaled,
        rows_block,
        (((0,), (0,)), ((), ())),
        precision=high,
        preferred_element_type=jnp.float32,
    )
    return (row_grad, col_grad)


def collect(received, slot_ids, blocks):
    onehot = (slot_ids[:, None] == jnp.arange(blocks, dtype=jnp.int32)[None, :]).astype(jnp.float32)
    return jnp.einsum("pmd,ms->psd", received, onehot, precision=lax.Precision.HIGHEST)


def body(
    row_table,
    col_table,
    row_accum,
    col_accum,
    row_margin,
    col_margin,
    row_blocks,
    col_blocks,
    slot_of,
    counts,
):
    per_device = row_blocks.shape[0]
    blocks = row_table.shape[1]
    row_all, col_all = (
        lax.all_gather(row_blocks, "dev", axis=0, tiled=True),
        lax.all_gather(col_blocks, "dev", axis=0, tiled=True),
    )
    row_slots = slot_of[row_all]
    col_slots = slot_of[col_all]
    send_rows = jnp.take(row_table, row_slots, axis=1)
    send_cols = jnp.take(col_table, col_slots, axis=1)
    send_mr = jnp.take(row_margin, row_slots, axis=1)
    send_mc = jnp.take(col_margin, col_slots, axis=1)
    got_rows, got_cols, got_mr, got_mc = (
        lax.all_to_all(send_rows, "dev", split_axis=1, concat_axis=0, tiled=True),
        lax.all_to_all(send_cols, "dev", split_axis=1, concat_axis=0, tiled=True),
        lax.all_to_all(send_mr, "dev", split_axis=1, concat_axis=0, tiled=True),
        lax.all_to_all(send_mc, "dev", split_axis=1, concat_axis=0, tiled=True),
    )
    row_parts = []
    col_parts = []
    for shard in range(per_device):
        row_grad, col_grad = shard_grads(
            got_rows[:, shard, :],
            got_cols[:, shard, :],
            got_mr[:, shard],
            got_mc[:, shard],
            counts[shard],
        )
        row_parts.append(row_grad)
        col_parts.append(col_grad)
    out_rows = jnp.stack(row_parts, axis=1)
    out_cols = jnp.stack(col_parts, axis=1)
    back_rows, back_cols = (
        lax.all_to_all(out_rows, "dev", split_axis=0, concat_axis=1, tiled=True),
        lax.all_to_all(out_cols, "dev", split_axis=0, concat_axis=1, tiled=True),
    )
    grad_rows = collect(back_rows, row_slots, blocks)
    grad_cols = collect(back_cols, col_slots, blocks)
    new_row_accum = row_accum + grad_rows * grad_rows
    new_col_accum = col_accum + grad_cols * grad_cols
    new_row_table = row_table - grad_rows / jnp.sqrt(new_row_accum)
    new_col_table = col_table - grad_cols / jnp.sqrt(new_col_accum)
    return (new_row_table, new_col_table, new_row_accum, new_col_accum)


def solution(mesh):
    return jax.shard_map(
        body,
        mesh=mesh,
        in_specs=(
            P("dev", None, None),
            P("dev", None, None),
            P("dev", None, None),
            P("dev", None, None),
            P("dev", None),
            P("dev", None),
            P("dev"),
            P("dev"),
            P(),
            P("dev", None, None),
        ),
        out_specs=(
            P("dev", None, None),
            P("dev", None, None),
            P("dev", None, None),
            P("dev", None, None),
        ),
        check_vma=False,
    )
```

profile of v0, /device:TPU:0, one launch (start us, length us, event | category | flops | bytes accessed | tf_op | source)
XLA Modules:
  0.0 547.3 jit_solution(2882682574503660919)
XLA Ops:
  0.6 0.0 copy-start
  0.7 0.9 dynamic-update-slice.1
  1.5 0.8 dynamic-update-slice
  2.4 42.0 %all-reduce.2 = (s32[64]{0:T(128)S(1)}, s32[64]{0:T(128)S(1)}) all-reduce(s32[64]{0:T(128)S(1)} %dynamic-update-slice.1, s32[64]{0:T(128)S(1)} %dynamic-update-slice), channel_id=1, replica_groups=mesh['dev'=32] {'dev'}, use_global_device_ids=true, to_apply=%add.1 | all-reduce | flops 128 | bytes 1024
  44.3 0.0 copy-done
  44.4 0.8 gather_fusion
  45.2 0.8 copy.40
  46.0 0.6 gather_fusion.4
  46.6 0.7 broadcast_select_fusion.1
  47.2 4.4 all-to-all-start.2
  51.7 0.8 gather_fusion.1
  52.5 0.8 copy.42
  53.3 0.6 gather_fusion.5
  53.9 0.7 broadcast_select_fusion
  54.6 9.4 %gather_fusion.3 = f32[64,32,512]{2,0,1:T(8,128)} fusion(f32[32,32,512]{2,1,0:T(8,128)} %param.15, s32[1024]{0:T(1024)S(1)} %pad_clamp_fusion), kind=kCustom, calls=%fused_computation.2.clone | custom fusion | bytes 8388864 | tf_op jit(solution)/shard_map/jit(_take)/gather | solution.py:54
  63.9 0.0 all-to-all-done.2
  63.9 5.8 %all-to-all-start.3 = ((f32[32,32,2]{0,2,1:T(2,128)}), f32[32,32,2]{0,2,1:T(2,128)S(1)}, u32[]{:S(2)}, u32[]{:S(2)}) async-start(f32[32,32,2]{0,2,1:T(2,128)} %bitcast.19), calls=%async_computation.3 | async-start | bytes 65536 | tf_op jit(solution)/shard_map/all_to_all | solution.py:61
  69.8 2.9 select_bitcast_fusion
  72.7 4.4 copy.38
  77.1 0.0 all-to-all-done.3
  77.1 6.4 %all-to-all-start.1 = ((f32[32,64,512]{2,0,1:T(8,128)}), f32[32,64,512]{2,0,1:T(8,128)}, u32[]{:S(2)}, u32[]{:S(2)}) async-start(f32[32,64,512]{2,0,1:T(8,128)} %copy.38), calls=%async_computation.1 | async-start | bytes 8388608 | tf_op jit(solution)/shard_map/all_to_all | solution.py:59
  83.5 0.0 copy-done.3
  83.5 8.4 %gather_fusion.2 = f32[64,32,512]{2,0,1:T(8,128)} fusion(f32[32,32,512]{2,1,0:T(8,128)S(1)} %copy-done.3, s32[1024]{0:T(1024)S(1)} %pad_clamp_fusion.2), kind=kCustom, calls=%fused_computation.clone | custom fusion | bytes 8388864 | tf_op jit(solution)/shard_map/jit(_take)/gather | solution.py:53
  91.9 2.9 select_bitcast_fusion.1
  94.8 4.4 copy.36
  99.3 78.2 %all-to-all-done.1 = f32[32,64,512]{2,0,1:T(8,128)} async-done(((f32[32,64,512]{2,0,1:T(8,128)}), f32[32,64,512]{2,0,1:T(8,128)}, u32[]{:S(2)}, u32[]{:S(2)}) %all-to-all-start.1) | async-done | bytes 4194336 | tf_op jit(solution)/shard_map/all_to_all | solution.py:59
  177.4 4.2 all-to-all-start
  181.7 0.1 all_to_all.91
  181.8 0.1 all_to_all.95
  181.9 5.0 copy.39
  186.9 88.7 %all-to-all-done = f32[32,64,512]{2,0,1:T(8,128)} async-done(((f32[32,64,512]{2,0,1:T(8,128)}), f32[32,64,512]{2,0,1:T(8,128)}, u32[]{:S(2)}, u32[]{:S(2)}) %all-to-all-start) | async-done | bytes 4194336 | tf_op jit(solution)/shard_map/all_to_all | solution.py:58
  275.6 2.8 copy.37
  278.4 0.6 copy-done.6
  279.0 18.2 %fusion.3 = f32[1024,1024]{1,0:T(8,128)S(1)} fusion(s32[2,1024,1024]{2,1,0:T(8,128)} %param.23, f32[1024]{0:T(1024)S(1)} %bitcast.147, f32[1024]{0:T(1024)S(1)} %bitcast.146, f32[1024,2,512]{2,0,1:T(8,128)S(1)} %bitcast.138, f32[1024,2,512]{2,0,1:T(8,128)S(1)} %bitcast.135), kind=kOutput, calls=%fused_computation.13 | convolution fusion | flops 6457131008 | bytes 12591104 | tf_op jit(solution)/shard_map/dot_general | solution.py:9
  297.3 0.0 copy-start.8
  297.3 6.8 %fusion.17 = f32[1024,1,512]{2,0,1:T(8,128)S(1)} fusion(f32[1024,1024]{1,0:T(8,128)S(1)} %fusion.3, f32[1024,2,512]{2,0,1:T(8,128)S(1)} %bitcast.139), kind=kOutput, calls=%fused_computation.41 | convolution fusion | flops 6442450944 | bytes 8388608 | tf_op jit(solution)/shard_map/dot_general | solution.py:18
  304.0 0.0 copy-done.8
  304.0 0.0 slice-done
  304.1 0.0 slice-done.1
  304.1 10.5 %fusion.7 = f32[1024,1024]{1,0:T(8,128)S(1)} fusion(s32[2,1024,1024]{2,1,0:T(8,128)S(1)} %bitcast.149, f32[1024]{0:T(1024)S(1)} %bitcast.145, f32[1024]{0:T(1024)S(1)} %bitcast.144, f32[1024,2,512]{2,0,1:T(8,128)S(1)} %bitcast.140, f32[1024,2,512]{2,0,1:T(8,128)S(1)} %bitcast.136), kind=kOutput, calls=%fused_computation.19 | convolution fusion | flops 6457131008 | bytes 12591104 | tf_op jit(solution)/shard_map/dot_general | solution.py:9
  314.5 0.0 copy-start.9
  314.6 6.8 %fusion.19 = f32[1024,1,512]{2,0,1:T(8,128)S(1)} fusion(f32[1024,1024]{1,0:T(8,128)S(1)} %fusion.7, f32[1024,2,512]{2,0,1:T(8,128)S(1)} %bitcast.141), kind=kOutput, calls=%fused_computation.43 | convolution fusion | flops 6442450944 | bytes 8388608 | tf_op jit(solution)/shard_map/dot_general | solution.py:18
  321.3 0.0 copy-done.9
  321.3 0.4 pad_maximum_fusion.1
  321.8 5.4 copy.46
  327.1 4.0 all-to-all-start.5
  331.2 0.0 copy-start.7
  331.2 0.0 copy-start.10
  331.2 9.4 %fusion.16 = f32[1024,1,512]{2,0,1:T(8,128)S(1)} fusion(f32[1024,1024]{1,0:T(8,128)} %copy-done.8, f32[1024,2,512]{2,0,1:T(8,128)} %bitcast.134), kind=kOutput, calls=%fused_computation.40 | convolution fusion | flops 6442450944 | bytes 8388608 | tf_op jit(solution)/shard_map/dot_general | solution.py:17
  340.7 6.7 %fusion.18 = f32[1024,1,512]{2,0,1:T(8,128)S(1)} fusion(f32[1024,1024]{1,0:T(8,128)S(1)} %copy-done.10, f32[1024,2,512]{2,0,1:T(8,128)S(1)} %bitcast.137), kind=kOutput, calls=%fused_computation.42 | convolution fusion | flops 6442450944 | bytes 8388608 | tf_op jit(solution)/shard_map/dot_general | solution.py:17
  347.4 0.4 pad_maximum_fusion
  347.8 5.2 copy.44
  353.1 72.0 %all-to-all-done.5 = f32[1024,2,512]{2,1,0:T(2,128)} async-done(((f32[1024,2,512]{2,1,0:T(2,128)}), f32[1024,2,512]{2,1,0:T(2,128)}, u32[]{:S(2)}, u32[]{:S(2)}) %all-to-all-start.5) | async-done | bytes 4194336 | tf_op jit(solution)/shard_map/all_to_all | solution.py:79
  425.1 4.3 all-to-all-start.4
  429.4 6.5 %copy.50 = f32[32,32,2,512]{3,2,0,1:T(2,128)} copy(f32[32,32,2,512]{3,2,1,0:T(2,128)} %bitcast.37) | data formatting | bytes 8388608 | tf_op jit(solution)/shard_map/all_to_all | solution.py:79
  435.9 6.1 %all_to_all.103 = f32[32,64,512]{2,1,0:T(8,128)} reshape(f32[32,32,2,512]{3,2,1,0:T(2,128)} %bitcast.132) | data formatting | bytes 8388608 | tf_op jit(solution)/shard_map/all_to_all | solution.py:79
  442.0 81.2 %all-to-all-done.4 = f32[1024,2,512]{2,1,0:T(2,128)} async-done(((f32[1024,2,512]{2,1,0:T(2,128)}), f32[1024,2,512]{2,1,0:T(2,128)}, u32[]{:S(2)}, u32[]{:S(2)}) %all-to-all-start.4) | async-done | bytes 4194336 | tf_op jit(solution)/shard_map/all_to_all | solution.py:78
  523.2 6.5 %copy.51 = f32[32,32,2,512]{3,2,0,1:T(2,128)} copy(f32[32,32,2,512]{3,2,1,0:T(2,128)} %bitcast.31) | data formatting | bytes 8388608 | tf_op jit(solution)/shard_map/all_to_all | solution.py:78
  529.8 6.2 %all_to_all.99 = f32[32,64,512]{2,1,0:T(8,128)} reshape(f32[32,32,2,512]{3,2,1,0:T(2,128)} %bitcast.133) | data formatting | bytes 8388608 | tf_op jit(solution)/shard_map/all_to_all | solution.py:78
  535.9 0.0 copy-done.2
  536.0 0.0 copy-start.11
  536.0 0.0 copy-start.1
  536.0 7.0 %fusion.9 = (f32[32,32,512]{2,1,0:T(8,128)}, f32[32,32,512]{2,1,0:T(8,128)}) fusion(f32[32,32,512]{2,1,0:T(8,128)S(1)} %copy-done.2, f32[32,32,512]{2,1,0:T(8,128)} %param.17, f32[32,64,512]{2,1,0:T(8,128)} %all_to_all.103, s32[64]{0:T(128)S(1)} %gather_fusion.1), kind=kOutput, calls=%fused_computation.31 | convolution fusion | flops 404752384 | bytes 12583168 | tf_op jit(solution)/shard_map/pmd,ms->psd/dot_general | solution.py:30
  543.0 4.1 fusion.11
  (29 shorter events, 0.1 us)
Async XLA Ops:
  0.6 43.7 %copy-start = (s32[32]{0:T(128)S(1)}, s32[32]{0:T(128)}, u32[]{:S(2)}) copy-start(s32[32]{0:T(128)} %param.22) | copy-start | bytes 388
  47.2 16.7 %all-to-all-start.2 = ((f32[32,32,2]{0,2,1:T(2,128)}), f32[32,32,2]{0,2,1:T(2,128)S(1)}, u32[]{:S(2)}, u32[]{:S(2)}) async-start(f32[32,32,2]{0,2,1:T(2,128)} %bitcast.15), calls=%async_computation.2 | async-start | bytes 65536 | tf_op jit(solution)/shard_map/all_to_all | solution.py:60
  63.9 13.2 %all-to-all-start.3 = ((f32[32,32,2]{0,2,1:T(2,128)}), f32[32,32,2]{0,2,1:T(2,128)S(1)}, u32[]{:S(2)}, u32[]{:S(2)}) async-start(f32[32,32,2]{0,2,1:T(2,128)} %bitcast.19), calls=%async_computation.3 | async-start | bytes 65536 | tf_op jit(solution)/shard_map/all_to_all | solution.py:61
  77.1 6.4 %copy-start.3 = (f32[32,32,512]{2,1,0:T(8,128)S(1)}, f32[32,32,512]{2,1,0:T(8,128)}, u32[]{:S(2)}) copy-start(f32[32,32,512]{2,1,0:T(8,128)} %param.14) | copy-start | bytes 6291460
  77.1 100.4 %all-to-all-start.1 = ((f32[32,64,512]{2,0,1:T(8,128)}), f32[32,64,512]{2,0,1:T(8,128)}, u32[]{:S(2)}, u32[]{:S(2)}) async-start(f32[32,64,512]{2,0,1:T(8,128)} %copy.38), calls=%async_computation.1 | async-start | bytes 8388608 | tf_op jit(solution)/shard_map/all_to_all | solution.py:59
  177.4 98.1 %all-to-all-start = ((f32[32,64,512]{2,0,1:T(8,128)}), f32[32,64,512]{2,0,1:T(8,128)}, u32[]{:S(2)}, u32[]{:S(2)}) async-start(f32[32,64,512]{2,0,1:T(8,128)} %copy.36), calls=%async_computation | async-start | bytes 8388608 | tf_op jit(solution)/shard_map/all_to_all | solution.py:58
  275.6 3.4 copy-start.6
  275.6 28.5 %slice-start = ((s8[8388608]{0:T(1024)(128)(4,1)}), s8[4194304]{0:T(1024)(128)(4,1)S(1)}, s32[]{:S(2)}) async-start(s8[8388608]{0:T(1024)(128)(4,1)} %bitcast.148), calls=%async_computation.6 | async-start | bytes 8388608
  279.0 25.0 %slice-start.1 = ((s8[8388608]{0:T(1024)(128)(4,1)}), s8[4194304]{0:T(1024)(128)(4,1)S(1)}, s32[]{:S(2)}) async-start(s8[8388608]{0:T(1024)(128)(4,1)} %bitcast.148), calls=%async_computation.7 | async-start | bytes 8388608
  297.3 6.8 %copy-start.8 = (f32[1024,1024]{1,0:T(8,128)}, f32[1024,1024]{1,0:T(8,128)S(1)}, u32[]{:S(2)}) copy-start(f32[1024,1024]{1,0:T(8,128)S(1)} %fusion.3) | copy-start | bytes 12582916
  314.5 6.8 %copy-start.9 = (f32[1024,1024]{1,0:T(8,128)}, f32[1024,1024]{1,0:T(8,128)S(1)}, u32[]{:S(2)}) copy-start(f32[1024,1024]{1,0:T(8,128)S(1)} %fusion.7) | copy-start | bytes 12582916
  327.1 97.9 %all-to-all-start.5 = ((f32[1024,2,512]{2,1,0:T(2,128)}), f32[1024,2,512]{2,1,0:T(2,128)}, u32[]{:S(2)}, u32[]{:S(2)}) async-start(f32[1024,2,512]{2,1,0:T(2,128)} %copy.46), calls=%async_computation.5 | async-start | bytes 8388608 | tf_op jit(solution)/shard_map/all_to_all | solution.py:79
  331.2 9.5 %copy-start.7 = (f32[32,32,2,512]{3,1,0,2:T(8,128)S(1)}, f32[32,32,2,512]{3,1,0,2:T(8,128)}, u32[]{:S(2)}) copy-start(f32[32,32,2,512]{3,1,0,2:T(8,128)} %copy.39) | copy-start | bytes 12582916
  331.2 9.5 %copy-start.10 = (f32[1024,1024]{1,0:T(8,128)S(1)}, f32[1024,1024]{1,0:T(8,128)}, u32[]{:S(2)}) copy-start(f32[1024,1024]{1,0:T(8,128)} %copy-done.9) | copy-start | bytes 12582916
  425.1 98.1 %all-to-all-start.4 = ((f32[1024,2,512]{2,1,0:T(2,128)}), f32[1024,2,512]{2,1,0:T(2,128)}, u32[]{:S(2)}, u32[]{:S(2)}) async-start(f32[1024,2,512]{2,1,0:T(2,128)} %copy.44), calls=%async_computation.4 | async-start | bytes 8388608 | tf_op jit(solution)/shard_map/all_to_all | solution.py:78
  529.8 6.2 %copy-start.2 = (f32[32,32,512]{2,1,0:T(8,128)S(1)}, f32[32,32,512]{2,1,0:T(8,128)}, u32[]{:S(2)}) copy-start(f32[32,32,512]{2,1,0:T(8,128)} %param.15) | copy-start | bytes 6291460
  535.9 7.1 %copy-start.4 = (f32[32,32,512]{2,1,0:T(8,128)S(1)}, f32[32,32,512]{2,1,0:T(8,128)}, u32[]{:S(2)}) copy-start(f32[32,32,512]{2,1,0:T(8,128)} %param.14) | copy-start | bytes 6291460
  535.9 7.1 %copy-start.5 = (f32[32,64,512]{2,1,0:T(8,128)S(1)}, f32[32,64,512]{2,1,0:T(8,128)}, u32[]{:S(2)}) copy-start(f32[32,64,512]{2,1,0:T(8,128)} %all_to_all.99) | copy-start | bytes 12582916
  536.0 7.1 %copy-start.11 = (f32[32,32,512]{2,1,0:T(8,128)S(1)}, f32[32,32,512]{2,1,0:T(8,128)}, u32[]{:S(2)}) copy-start(f32[32,32,512]{2,1,0:T(8,128)} %param.16) | copy-start | bytes 6291460
  536.0 11.1 %copy-start.1 = (s32[32]{0:T(128)S(1)}, s32[32]{0:T(128)}, u32[]{:S(2)}) copy-start(s32[32]{0:T(128)} %param.22) | copy-start | bytes 388
where the time goes:
time: 554 us; the launch traced here: 547 us
  waiting for transfers between devices  320 us (58%)
  local copies, waits for them, and re-layouts  77.2 us (14%)
  matrix products  69.5 us (13%)
  blocking collectives  42 us (8%)
  starting transfers between devices  29.2 us (5%)
  other arithmetic  8.14 us (1%)
    all_to_all x1, waiting for transfers between devices, body(): lax.all_to_all(send_rows, 'dev', split_axis=1, concat_axis=0, tiled=True)  88.7 us
    all_to_all x1, waiting for transfers between devices, body(): lax.all_to_all(out_rows, 'dev', split_axis=0, concat_axis=1, tiled=True)  81.2 us
    all_to_all x1, waiting for transfers between devices, body(): lax.all_to_all(send_cols, 'dev', split_axis=1, concat_axis=0, tiled=True)  78.2 us
    all_to_all x1, waiting for transfers between devices, body(): lax.all_to_all(out_cols, 'dev', split_axis=0, concat_axis=1, tiled=True)  72 us
    unnamed x1, blocking collectives  42 us
    dot_general x2, matrix products, shard_grads(): jnp.dot(rows_block, cols_block.T, precision=high, preferred_element_type=...  28.7 us
    dot_general x2, matrix products, shard_grads(): jnp.dot(scaled, cols_block, precision=high, preferred_element_type=jnp.fl...  16.1 us
    dot_general x2, matrix products, shard_grads(): lax.dot_general(scaled, rows_block, (((0,), (0,)), ((), ())), precision=h...  13.5 us
  transfers between devices with their start and end apart: 6, of which 4 were waited for; matrix products, arithmetic and copies ran while one was open for 13% of the time, Pallas kernels for 0%

commit v1 on v0

v1 whole, which is shorter than its diff:
```python
import functools

import jax
import jax.numpy as jnp
from jax import lax
from jax.experimental import pallas as pl
from jax.experimental.pallas import tpu as pltpu
from jax.sharding import PartitionSpec as P

LEAST_GROUP = 32
LANES = 128
VMEM_LIMIT = 56 * 1024 * 1024
F32 = jnp.float32
BF16 = jnp.bfloat16
COST = pl.CostEstimate(flops=1, bytes_accessed=1, transcendentals=0)


def params():
    return pltpu.CompilerParams(vmem_limit_bytes=VMEM_LIMIT)


def lowest_bit(unit):
    return (unit & -unit).bit_length() - 1


def split(x):
    hi = x.astype(BF16)
    return hi, (x - hi.astype(F32)).astype(BF16)


def dot3(a_hi, a_lo, b_hi, b_lo, dims):
    def dot(a, b):
        return lax.dot_general(a, b, (dims, ((), ())), preferred_element_type=F32)

    return dot(a_hi, b_hi) + dot(a_hi, b_lo) + dot(a_lo, b_hi)


def block_major_kernel(row_ref, col_ref, out_ref):
    tiles = pl.num_programs(0) // 2

    @pl.when(pl.program_id(0) < tiles)
    def _():
        out_ref[...] = jnp.swapaxes(row_ref[...], 0, 1)

    @pl.when(pl.program_id(0) >= tiles)
    def _():
        out_ref[...] = jnp.swapaxes(col_ref[...], 0, 1)


def block_major(row_table, col_table):
    pos, blocks, width = row_table.shape
    tiles = blocks // 8
    return pl.pallas_call(
        block_major_kernel,
        grid=(2 * tiles,),
        in_specs=[
            pl.BlockSpec((pos, 8, width), lambda i: (0, jnp.minimum(i, tiles - 1), 0)),
            pl.BlockSpec((pos, 8, width), lambda i: (0, jnp.maximum(i - tiles, 0), 0)),
        ],
        out_specs=pl.BlockSpec((8, pos, width), lambda i: (i, 0, 0)),
        out_shape=jax.ShapeDtypeStruct((2 * blocks, pos, width), F32),
        compiler_params=params(),
        cost_estimate=COST,
        name="block_major",
    )(row_table, col_table)


def pick_kernel(plans, scalars, sources, *refs):
    scalar_refs = refs[:scalars]
    src_refs = refs[scalars : scalars + sources]
    out_refs = refs[scalars + sources :]
    for out_ref, pieces in zip(out_refs, plans):
        for source, index, table, at_unit, lanes in pieces:
            src_ref, index_ref = src_refs[source], scalar_refs[index]
            table_ref = None if table is None else scalar_refs[table]
            start, stop = lanes
            if at_unit is None:

                def step(j, carry, src_ref=src_ref, index_ref=index_ref, table_ref=table_ref, out_ref=out_ref, start=start, stop=stop):
                    at = index_ref[j]
                    at = at if table_ref is None else table_ref[at]
                    out_ref[j] = src_ref[at, :, start:stop]
                    return carry

                lax.fori_loop(0, out_ref.shape[0], step, 0)
            else:
                named = out_ref.shape[2]

                def step(j, carry, src_ref=src_ref, index_ref=index_ref, table_ref=table_ref, out_ref=out_ref, at_unit=at_unit, named=named):
                    for k in range(named):
                        at = index_ref[j * named + k]
                        at = at if table_ref is None else table_ref[at]
                        out_ref[j, at_unit, k] = src_ref[at]
                    return carry

                lax.fori_loop(0, out_ref.shape[0], step, 0)


def pick(sources, outputs):
    scalars, plans = [], []

    def number(x):
        for at, known in enumerate(scalars):
            if known is x:
                return at
        scalars.append(x)
        return len(scalars) - 1

    for shape, pieces in outputs:
        plan = []
        for source, index, table, unit, lanes in pieces:
            lanes = (0, shape[-1]) if lanes is None else lanes
            plan.append((source, number(index), None if table is None else number(table), unit, lanes))
        plans.append(tuple(plan))
    zeros = lambda shape: lambda i, *_: (0,) * len(shape)
    return pl.pallas_call(
        functools.partial(pick_kernel, tuple(plans), len(scalars), len(sources)),
        grid_spec=pltpu.PrefetchScalarGridSpec(
            num_scalar_prefetch=len(scalars),
            grid=(1,),
            in_specs=[pl.BlockSpec(x.shape, zeros(x.shape)) for x in sources],
            out_specs=[pl.BlockSpec(shape, zeros(shape)) for shape, _ in outputs],
        ),
        out_shape=[jax.ShapeDtypeStruct(shape, F32) for shape, _ in outputs],
        compiler_params=params(),
        cost_estimate=COST,
        name="pick",
    )(*scalars, *sources)


def place_kernel(plans, *refs):
    scalars = refs[: 2 * len(plans)]
    sources = refs[2 * len(plans) : -1]
    out_ref = refs[-1]
    out_ref[...] = jnp.zeros_like(out_ref)
    at_source = 0
    for number, (count, mapped, lanes) in enumerate(plans):
        index_ref, map_ref = scalars[2 * number], scalars[2 * number + 1]
        for start, stop in lanes:
            src_ref = sources[at_source]
            at_source += 1
            named = src_ref.shape[2] if len(src_ref.shape) == 5 else 1

            def step(j, carry, src_ref=src_ref, index_ref=index_ref, map_ref=map_ref, mapped=mapped, start=start, stop=stop, named=named):
                for k in range(named):
                    at = index_ref[j * named + k]
                    at = map_ref[at] if mapped else at
                    block = src_ref[j, 0, k] if len(src_ref.shape) == 5 else src_ref[j]
                    out_ref[at, :, start:stop] += block
                return carry

            lax.fori_loop(0, count // named, step, 0)


def place(terms, count):
    plans, scalars, sources, specs = [], [], [], []
    for arrays, index, table in terms:
        lanes, at = [], 0
        for array, unit in arrays:
            lanes.append((at, at + array.shape[-1]))
            at += array.shape[-1]
            sources.append(array)
            if array.ndim == 5:
                group, _, named, pos, part = array.shape
                entries = group * named
                specs.append(pl.BlockSpec((group, 1, named, pos, part), lambda i, *_, unit=unit: (0, unit, 0, 0, 0)))
            else:
                entries, pos, _ = array.shape
                specs.append(pl.BlockSpec(array.shape, lambda i, *_: (0, 0, 0)))
        plans.append((entries, table is not None, tuple(lanes)))
        scalars += [index, index if table is None else table]
        width = at
    return pl.pallas_call(
        functools.partial(place_kernel, tuple(plans)),
        grid_spec=pltpu.PrefetchScalarGridSpec(
            num_scalar_prefetch=len(scalars),
            grid=(1,),
            in_specs=specs,
            out_specs=pl.BlockSpec((count, pos, width), lambda i, *_: (0, 0, 0)),
        ),
        out_shape=jax.ShapeDtypeStruct((count, pos, width), F32),
        compiler_params=params(),
        cost_estimate=COST,
        name="place",
    )(*scalars, *sources)


def scaled_kernel(pieces, planes, plane_ref, *refs):
    count = len(pieces)
    row_refs, col_refs = refs[:count], refs[count : 2 * count]
    counts_ref, u_ref, v_ref = refs[2 * count : 2 * count + 3]
    s_hi, s_lo, r_hi, r_lo, c_hi, c_lo = refs[2 * count + 3 :]
    step = pl.program_id(1)
    plane = plane_ref[0]
    rows = s_hi.shape[1]
    size = s_hi.shape[2]
    tile = size // planes

    @pl.when(step == 0)
    def _():
        for number, (unit, start, stop) in enumerate(pieces):
            at = pl.multiple_of(lax.bitwise_xor(plane, unit) * tile, tile)
            for src, hi_ref, lo_ref in ((row_refs[number], r_hi, r_lo), (col_refs[number], c_hi, c_lo)):
                hi, lo = split(src[...].reshape(tile, stop - start))
                hi_ref[0, pl.ds(at, tile), start:stop] = hi
                lo_ref[0, pl.ds(at, tile), start:stop] = lo

    mine = pl.ds(pl.multiple_of(step * rows, rows), rows)
    logits = dot3(r_hi[0, mine, :], r_lo[0, mine, :], c_hi[0], c_lo[0], ((1,), (1,)))
    tile_counts = counts_ref[0]
    values = tile_counts.astype(F32)
    target = jnp.log(jnp.maximum(values, 1.0)) - u_ref[0] - v_ref[0]
    error = logits - target
    confidence = 0.1 + 0.25 * jnp.sqrt(values)
    scaled = jnp.where(tile_counts > 0, confidence * error, jax.nn.sigmoid(error)) * (1.0 / size)
    hi, lo = split(scaled)
    s_hi[0] = hi
    s_lo[0] = lo


def scaled_parts(pieces, counts, u, v, plane, planes, first=0, shards=None):
    every, size, _ = counts.shape
    shards = shards or every
    steps = max(planes, 4)
    rows = size // steps
    layout = tuple((unit, first, first + array.shape[4]) for unit, array, _, first in pieces)
    width = max(stop for _, _, stop in layout)
    in_specs = []
    for kind in (0, 1):
        for _, array, at, _ in pieces:
            group, _, _, pos, part = array.shape
            in_specs.append(
                pl.BlockSpec((group, 1, 1, pos, part), lambda s, i, z, kind=kind, at=at: (0, at, 2 * s + kind, 0, 0))
            )
    arrays = [array for _, array, _, _ in pieces]
    in_specs += [
        pl.BlockSpec((1, rows, size), lambda s, i, z: (s + first, i, 0)),
        pl.BlockSpec((1, rows, 1), lambda s, i, z: (s + first, i, 0)),
        pl.BlockSpec((1, 1, size), lambda s, i, z: (s + first, 0, 0)),
    ]
    tile_spec = pl.BlockSpec((1, rows, size), lambda s, i, z: (s, i, 0))
    whole_spec = pl.BlockSpec((1, size, width), lambda s, i, z: (s, 0, 0))
    return pl.pallas_call(
        functools.partial(scaled_kernel, layout, planes),
        grid_spec=pltpu.PrefetchScalarGridSpec(
            num_scalar_prefetch=1,
            grid=(shards, steps),
            in_specs=in_specs,
            out_specs=[tile_spec] * 2 + [whole_spec] * 4,
        ),
        out_shape=[jax.ShapeDtypeStruct((shards, size, size), BF16)] * 2
        + [jax.ShapeDtypeStruct((shards, size, width), BF16)] * 4,
        compiler_params=params(),
        cost_estimate=COST,
        name="scaled",
    )(plane, *arrays, *arrays, counts, u, v)


def grads_kernel(units, plane_ref, *refs):
    tiles, (r_hi, r_lo, c_hi, c_lo, out_ref) = refs[: 4 * units], refs[4 * units :]
    group, _, _, pos, part = out_ref.shape
    for at in range(units):
        sr_hi, sr_lo, sc_hi, sc_lo = tiles[4 * at : 4 * at + 4]
        row_grad = dot3(sr_hi[0], sr_lo[0], c_hi[0], c_lo[0], ((1,), (0,)))
        out_ref[:, at, 0] = row_grad.reshape(group, pos, part)
        col_grad = dot3(sc_hi[0], sc_lo[0], r_hi[0], r_lo[0], ((0,), (0,)))
        out_ref[:, at, 1] = col_grad.reshape(group, pos, part)


def grads(parts, plane, units, chunk, chunks, planes, group, pos):
    s_hi, s_lo, r_hi, r_lo, c_hi, c_lo = parts
    shards, size, width = r_hi.shape
    tile, part = size // planes, width // chunks
    specs = []
    for unit in units:
        rows = pl.BlockSpec((1, tile, size), lambda s, z, unit=unit: (s, lax.bitwise_xor(z[0], unit), 0))
        cols = pl.BlockSpec((1, size, tile), lambda s, z, unit=unit: (s, 0, lax.bitwise_xor(z[0], unit)))
        specs += [rows, rows, cols, cols]
    block = pl.BlockSpec((1, size, part), lambda s, z: (s, 0, chunk))
    return pl.pallas_call(
        functools.partial(grads_kernel, len(units)),
        grid_spec=pltpu.PrefetchScalarGridSpec(
            num_scalar_prefetch=1,
            grid=(shards,),
            in_specs=specs + [block] * 4,
            out_specs=pl.BlockSpec((group, len(units), 2, pos, part), lambda s, z: (0, 0, s, 0, 0)),
        ),
        out_shape=jax.ShapeDtypeStruct((group, len(units), 2 * shards, pos, part), F32),
        compiler_params=params(),
        cost_estimate=COST,
        name="grads",
    )(plane, *([s_hi, s_lo, s_hi, s_lo] * len(units)), r_hi, r_lo, c_hi, c_lo)


def update_kernel(grad_ref, table_ref, accum_ref, new_table_ref, new_accum_ref):
    grad = jnp.swapaxes(grad_ref[...], 0, 1)
    accum = accum_ref[...] + grad * grad
    new_accum_ref[...] = accum
    new_table_ref[...] = table_ref[...] - grad / jnp.sqrt(accum)


def update(grad, table, accum, first):
    pos, blocks, width = table.shape
    spec = pl.BlockSpec((pos, 8, width), lambda i: (0, i, 0))
    return pl.pallas_call(
        update_kernel,
        grid=(blocks // 8,),
        in_specs=[pl.BlockSpec((8, pos, width), lambda i: (i + first // 8, 0, 0)), spec, spec],
        out_specs=[spec, spec],
        out_shape=[jax.ShapeDtypeStruct(table.shape, F32)] * 2,
        compiler_params=params(),
        cost_estimate=COST,
        name="update",
    )(grad, table, accum)


def body(
    row_table, col_table, row_accum, col_accum, row_margin, col_margin, row_blocks, col_blocks, slot_of, counts, *, devices
):
    planes = min(devices // LEAST_GROUP, counts.shape[1] // LANES)
    group = devices // planes
    stages = planes.bit_length() - 1
    shards = row_blocks.shape[0]
    pos, blocks, width = row_table.shape
    size = counts.shape[1]
    slots = 2 * blocks
    named = 2 * shards
    plane = lax.axis_index("dev") // group
    groups = [[group * z + c for c in range(group)] for z in range(planes)]

    def across(x, stage):
        return lax.ppermute(x, "dev", [(d, d ^ (group << stage)) for d in range(devices)])

    def inside(x):
        return lax.all_to_all(x, "dev", 0, 0, axis_index_groups=groups, tiled=True)

    own_ids = jnp.stack([row_blocks, col_blocks], axis=1)
    every = jnp.arange(blocks, dtype=jnp.int32)
    own_slots = jnp.sum(jnp.where(own_ids[:, :, None] == every, slot_of, 0), axis=2)
    own_slots = (own_slots + jnp.array([0, blocks], jnp.int32)).reshape(named).astype(F32)
    margins = jnp.concatenate([row_margin, col_margin], axis=1).reshape(-1)
    told = jnp.concatenate([jnp.pad(own_slots, (0, LANES - named)), margins])
    told = lax.all_to_all(jnp.broadcast_to(told, (devices, told.shape[0])), "dev", 0, 0, tiled=True)
    named_slots = told[:, :named].astype(jnp.int32)

    tables = block_major(row_table, col_table)

    every = jnp.arange(slots, dtype=jnp.int32)
    member = jnp.any(named_slots[:, :, None] == every, axis=1)
    upto = (every[:, None] <= every[None, :]).astype(F32)
    lists, ranks, most = [], [], []
    for stage in range(stages):
        held = jnp.any(member.reshape(planes >> stage, group << stage, slots), axis=1)
        rank = jnp.dot(held.astype(F32), upto, preferred_element_type=F32).astype(jnp.int32) - 1
        most.append(jnp.max(rank[:, -1]) + 1)
        cap = min(slots, named * (group << stage))
        theirs = lax.bitwise_xor(plane, 1 << stage) >> stage
        their_held = lax.dynamic_index_in_dim(held, theirs, 0, keepdims=False)
        their_rank = lax.dynamic_index_in_dim(rank, theirs, 0, keepdims=False)
        hit = (their_rank[None, :] == jnp.arange(cap, dtype=jnp.int32)[:, None]) & their_held[None, :]
        lists.append(jnp.sum(jnp.where(hit, every[None, :], 0), axis=1))
        ours = lax.dynamic_index_in_dim(rank, plane >> stage, 0, keepdims=False)
        ranks.append(jnp.maximum(ours, 0))
    entries = lax.dynamic_slice_in_dim(named_slots, plane * group, group, 0).reshape(group * named)
    plane_arg = plane.reshape(1).astype(jnp.int32)

    def margins_of(told):
        margins = told[:, LANES:].reshape(size, slots)
        mine = lax.dynamic_index_in_dim(named_slots, lax.axis_index("dev"), 0, keepdims=False)
        margins = jnp.sum(jnp.where(mine[:, None, None] == every, margins, 0.0), axis=2).reshape(shards, 2, size)
        return margins[:, 0, :, None], margins[:, 1, None, :]

    def direct(tables, told):
        shape = (group, 1, 2, pos, width)
        u, v = margins_of(told)
        got, index = [], []
        for shard in range(shards):
            index.append(named_slots[:, 2 * shard : 2 * shard + 2].reshape(2 * group))
            after = lax.optimization_barrier((index[-1], *got))[0] if got else index[-1]
            (sent,) = pick([tables], [(shape, [(0, after, None, 0, None)])])
            got.append(inside(sent))
        terms = []
        for shard in range(shards):
            parts = scaled_parts([(0, got[shard], 0, 0)], counts, u, v, plane_arg, planes, shard, 1)
            grad = grads(parts, plane_arg, (0,), 0, 1, planes, group, pos)
            terms.append(([(inside(grad), 0)], index[shard], None))
        grad = place(terms, slots)
        new_row_table, new_row_accum = update(grad, row_table, row_accum, 0)
        new_col_table, new_col_accum = update(grad, col_table, col_accum, blocks)
        return (new_row_table, new_col_table, new_row_accum, new_col_accum)

    if planes == 1:
        return direct(tables, told)

    def step(caps, tables, told):
        def table_of(unit):
            return None if unit == 0 else ranks[lowest_bit(unit)]

        before = []

        def gate(small, *waits):
            return lax.optimization_barrier((small, *before, *waits))[0] if before or waits else small

        def ran(x):
            before[:] = [x]
            return x

        def swap(x, work=lambda: ()):
            if planes != 4:
                return inside(x), work()
            got, done = lax.cond(most[0] > 0, lambda y: (inside(y), work()), lambda y: (y, work()), x)
            return ran(got), done

        source, pieces = {}, []
        def spread(unit, chunk, chunks):
            part = width // chunks
            shape = (group, 1, named, pos, part)
            (sent,) = pick([source[unit, chunk]], [(shape, [(0, gate(entries), table_of(unit), 0, None)])])
            got, _ = swap(ran(sent))
            pieces.append((unit, got, 0, chunk * part))

        source[0, 0] = tables
        chunks = 2 if planes == 4 else 1
        part = width // chunks
        if planes == 4:

            held = []

            def bring(chunk):
                lanes = (chunk * part, (chunk + 1) * part)
                near, far = pick(
                    [tables],
                    [
                        ((caps[0], pos, part), [(0, gate(lists[0]), None, None, lanes)]),
                        ((caps[1], pos, part), [(0, lists[1], None, None, lanes)]),
                    ],
                )
                ran(near)
                held.append((chunk, near, far))

            def leave(*waits):
                for chunk, near, far in held:
                    if waits:
                        near, far, *_ = lax.optimization_barrier((near, far, *waits))
                    source[1, chunk] = across(near, 0)
                    source[2, chunk] = across(far, 1)
                held.clear()

            def relay(chunk):
                (sent,) = pick([source[2, chunk]], [((caps[0], pos, part), [(0, gate(lists[0]), ranks[1], None, None)])])
                source[3, chunk] = across(ran(sent), 0)

            def spread_far(chunk):
                index = gate(entries)
                shape = (group, 2, named, pos, part)
                (sent,) = pick(
                    [source[2, chunk], source[3, chunk]],
                    [(shape, [(0, index, ranks[1], 0, None), (1, index, ranks[0], 1, None)])],
                )
                got, _ = swap(ran(sent))
                pieces.append((2, got, 0, chunk * part))
                pieces.append((3, got, 1, chunk * part))

            bring(0)
            leave()
            bring(1)
            spread(0, 0, 1)
            leave(*before, source[1, 0])
            spread(1, 0, 2)
            relay(0)
            spread(2, 0, 2)
            spread(1, 1, 2)
            relay(1)
            spread(3, 0, 2)
            spread_far(1)
        else:
            for stage in reversed(range(stages)):
                for unit in range(0, planes, 2 << stage):
                    shape = (caps[stage], pos, width)
                    (sent,) = pick([source[unit, 0]], [(shape, [(0, lists[stage], table_of(unit), None, None)])])
                    source[unit ^ (1 << stage), 0] = across(sent, stage)
            for unit in range(planes):
                spread(unit, 0, 1)

        u, v = margins_of(told)
        parts = scaled_parts(pieces, counts, u, v, plane_arg, planes)
        ran(parts[0])

        arrived, passed = {}, {}

        def differentiate(units, chunk, chunks):
            return grads(parts, gate(plane_arg), units, chunk, chunks, planes, group, pos)

        def swap_back(grad, units, chunk, after=None):
            work = (lambda: differentiate(*after)) if after else (lambda: ())
            got, following = swap(grad, work)
            for at, unit in enumerate(units):
                arrived[unit, chunk] = (got, at)
            return following

        def give(unit, chunk, *waits):
            stage = lowest_bit(unit)
            terms = [([arrived[unit, chunk]], gate(entries, *waits), ranks[stage])]
            for lower in range(stage):
                terms.append(([(passed[unit ^ (1 << lower), chunk], 0)], lists[lower], ranks[stage]))
            passed[unit, chunk] = across(ran(place(terms, caps[stage])), stage)

        if planes == 4:
            order = [((3,), 0, 2), ((2,), 0, 2), ((2, 3), 1, 2), ((1,), 0, 2), ((1,), 1, 2), ((0,), 0, 1), None]
            grad = ran(differentiate(*order[0]))
            for at, (units, chunk, _) in enumerate(order[:-1]):
                grad = swap_back(grad, units, chunk, order[at + 1])
                if at == 0:
                    give(3, 0)
                elif at == 1:
                    give(2, 0)
                elif at == 2:
                    give(3, 1)
                elif at == 3:
                    give(2, 1, passed[2, 0])
                    give(1, 0)
                elif at == 4:
                    give(1, 1, passed[1, 0])
        else:
            for unit in reversed(range(planes)):
                swap_back(ran(differentiate((unit,), 0, 1)), (unit,), 0)
            for stage in range(stages):
                for unit in reversed(range(1, planes)):
                    if lowest_bit(unit) == stage:
                        give(unit, 0)
        terms = [([arrived[0, 0]], entries, None)]
        for stage in range(stages):
            arrays = [(passed[1 << stage, chunk], 0) for chunk in range(4) if (1 << stage, chunk) in passed]
            terms.append((arrays, lists[stage], None))
        grad = place(terms, slots)
        new_row_table, new_row_accum = update(grad, row_table, row_accum, 0)
        new_col_table, new_col_accum = update(grad, col_table, col_accum, blocks)
        return (new_row_table, new_col_table, new_row_accum, new_col_accum)

    largest = tuple(min(slots, named * (group << stage)) for stage in range(stages))
    levels = [largest]
    if planes == 4:
        levels = [(largest[0] * k // 64, largest[1] * n // 64) for k, n in ((44, 32), (48, 34), (52, 38))] + levels
    if len(levels) == 1:
        return step(levels[0], tables, told)
    level = jnp.int32(0)
    for caps in levels[:-1]:
        fits = jnp.bool_(True)
        for cap, need in zip(caps, most):
            fits = fits & (need <= cap)
        level = level + jnp.where(fits, 0, 1)
    return lax.switch(level, [functools.partial(step, caps) for caps in levels], tables, told)


def solution(mesh):
    spec = P("dev", None, None)
    flat = P("dev", None)
    return jax.shard_map(
        functools.partial(body, devices=mesh.shape["dev"]),
        mesh=mesh,
        in_specs=(spec, spec, spec, spec, flat, flat, P("dev"), P("dev"), P(), spec),
        out_specs=(spec, spec, spec, spec),
        check_vma=False,
    )
```

time: 554 us -> 444 us (0.80); the launches traced: 547 us -> 443 us
  waiting for transfers between devices: 320 us -> 234 us
  Pallas kernels: 0 us -> 84.3 us
  local copies, waits for them, and re-layouts: 77.2 us -> 4.83 us
  matrix products: 69.5 us -> 0 us
  blocking collectives: 42 us -> 97.6 us
  starting transfers between devices: 29.2 us -> 19.1 us
    all_to_all x0 -> x1, blocking collectives: none -> 97.6 us  [inside(): return lax.all_to_all(x, 'dev', 0, 0, axis_index_groups=groups, tiled=True)]
    all_to_all x6 -> x4, waiting for transfers between devices: 320 us -> 234 us  [the longest x3 230 us: inside(): return lax.all_to_all(x, 'dev', 0, 0, axis_index_groups=groups, tiled=True)]
    pallas_call x0 -> x10, Pallas kernels: none -> 84.3 us  [the longest x2 26.4 us: grads(): pl.pallas_call(functools.partial(grads_kernel, len(units)), grid_spec=plt...]
    dot_general x8 -> x0, matrix products: 69.5 us -> none  [the longest x2 28.7 us: shard_grads(): jnp.dot(rows_block, cols_block.T, precision=high, preferred_element_type=...]
    unnamed x1 -> x0, blocking collectives: 42 us -> none
    all_to_all x10 -> x0, local copies, waits for them, and re-layouts: 33.4 us -> none  [the longest x2 12.7 us: body(): lax.all_to_all(out_rows, 'dev', split_axis=0, concat_axis=1, tiled=True)]
    gather x6 -> x0, local copies, waits for them, and re-layouts: 20.5 us -> none  [the longest x1 9.36 us: body(): send_cols = jnp.take(col_table, col_slots, axis=1)]
    all_to_all x6 -> x4, starting transfers between devices: 29.2 us -> 19.1 us  [the longest x3 11.8 us: inside(): return lax.all_to_all(x, 'dev', 0, 0, axis_index_groups=groups, tiled=True)]
  transfers between devices with their start and end apart: 6 -> 4, of which waited for: 4 -> 4; matrix products, arithmetic and copies ran while one was open for 13% -> 1% of each run, Pallas kernels for 0% -> 13%
where the time goes in v1:
time: 444 us; the launch traced here: 443 us
  waiting for transfers between devices  234 us (53%)
  blocking collectives  97.6 us (22%)
  Pallas kernels  84.3 us (19%)
  starting transfers between devices  19.1 us (4%)
  local copies, waits for them, and re-layouts  4.83 us (1%)
    all_to_all x3, waiting for transfers between devices, inside(): return lax.all_to_all(x, 'dev', 0, 0, axis_index_groups=groups, tiled=True)  230 us
    all_to_all x1, blocking collectives, inside(): return lax.all_to_all(x, 'dev', 0, 0, axis_index_groups=groups, tiled=True)  97.6 us
    pallas_call x2, Pallas kernels, grads(): pl.pallas_call(functools.partial(grads_kernel, len(units)), grid_spec=plt...  26.4 us
    pallas_call x2, Pallas kernels, scaled_parts(): pl.pallas_call(functools.partial(scaled_kernel, layout, planes), grid_spe...  22.2 us
    all_to_all x3, starting transfers between devices, inside(): return lax.all_to_all(x, 'dev', 0, 0, axis_index_groups=groups, tiled=True)  11.8 us
    pallas_call x2, Pallas kernels, update(): pl.pallas_call(update_kernel, grid=(blocks // 8,), in_specs=[pl.BlockSpec...  10.5 us
    pallas_call x2, Pallas kernels, pick(): pl.pallas_call(functools.partial(pick_kernel, tuple(plans), len(scalars),...  10.4 us
  transfers between devices with their start and end apart: 4, of which 4 were waited for; matrix products, arithmetic and copies ran while one was open for 1% of the time, Pallas kernels for 13%

profile of v1, /device:TPU:0, one launch (start us, length us, event | category | flops | bytes accessed | tf_op | source)
XLA Modules:
  0.0 442.9 jit_solution(8217578517734876974)
XLA Ops:
  0.6 0.7 pad_add_fusion
  1.3 0.1 copy.24
  1.4 0.9 fusion
  2.3 0.1 convert_element_type.12
  2.4 0.8 pad_maximum_fusion
  3.2 0.1 reshape.62
  3.3 0.9 broadcast_in_dim.34
  4.1 7.3 %all-to-all-start = ((f32[32,1,2176]{2,1,0:T(1,128)}), f32[32,1,2176]{2,1,0:T(1,128)S(1)}, u32[]{:S(2)}, u32[]{:S(2)}) async-start(f32[32,1,2176]{2,1,0:T(1,128)} %broadcast_in_dim.34), calls=%async_computation | async-start | bytes 557056 | tf_op jit(solution)/shard_map/all_to_all | solution.py:343
  11.4 7.2 %block_major.1.refs_1_ = f32[64,32,512]{2,1,0:T(8,128)} custom-call(f32[32,32,512]{2,1,0:T(8,128)} %table_ref.2, f32[32,32,512]{2,1,0:T(8,128)} %table_ref.3), custom_call_target="tpu_custom_call" | custom-call | flops 1 | bytes 1 | tf_op jit(solution)/shard_map/block_major/pallas_call | solution.py:53
  18.7 3.9 all-to-all-done
  22.6 0.1 fusion.2
  22.6 0.6 reshape.63.refs_0_.refs_1_
  23.3 5.2 %pick.2 = f32[32,1,2,32,512]{4,3,2,1,0:T(8,128)} custom-call(s32[64]{0:T(128)} %reshape.63.refs_0_.refs_1_, f32[64,32,512]{2,1,0:T(8,128)} %block_major.1.refs_1_), custom_call_target="tpu_custom_call" | custom-call | flops 1 | bytes 1 | tf_op jit(solution)/shard_map/pick/pallas_call | solution.py:116
  28.5 3.6 all-to-all-start.1
  32.1 0.6 reshape.64.refs_0_.refs_2_.refs_3_
  32.7 93.4 %all-to-all-done.1.refs_0_.refs_1_ = f32[32,1,2,32,512]{4,3,2,1,0:T(8,128)} async-done(((f32[32,1,2,32,512]{4,3,2,1,0:T(8,128)}), f32[32,1,2,32,512]{4,3,2,1,0:T(8,128)}, u32[]{:S(2)}, u32[]{:S(2)}) %all-to-all-start.1) | async-done | bytes 4194336 | tf_op jit(solution)/shard_map/all_to_all | solution.py:335
  126.1 5.2 %pick.3 = f32[32,1,2,32,512]{4,3,2,1,0:T(8,128)} custom-call(s32[64]{0:T(128)} %reshape.64.refs_0_.refs_2_.refs_3_, f32[64,32,512]{2,1,0:T(8,128)} %block_major.1.refs_1_), custom_call_target="tpu_custom_call" | custom-call | flops 1 | bytes 1 | tf_op jit(solution)/shard_map/pick/pallas_call | solution.py:116
  131.3 3.9 all-to-all-start.3
  135.3 0.2 reshape.66
  135.5 0.2 copy.25
  135.7 0.1 iota_compare_fusion.1
  135.8 0.2 select_reduce_fusion
  136.0 0.6 fusion.1
  136.6 1.3 copy.26.refs_3_
  138.0 10.9 %scaled.2 = (bf16[1,1024,1024]{2,1,0:T(8,128)(2,1)}, bf16[1,1024,1024]{2,1,0:T(8,128)(2,1)}, bf16[1,1024,512]{2,1,0:T(8,128)(2,1)}, bf16[1,1024,512]{2,1,0:T(8,1...) custom-call(s32[1]{0:T(128)} %bitcast.2.plane_ref, ...), custom_call_target="tpu_custom_call" | custom-call | flops 1 | bytes 1 | tf_op jit(solution)/shard_map/scaled/pallas_call | solution.py:243
  148.8 13.2 %grads.2 = f32[32,1,2,32,512]{4,3,2,1,0:T(8,128)} custom-call(s32[1]{0:T(128)} %bitcast.2.plane_ref, bf16[1,1024,1024]{2,1,0:T(8,128)(2,1)} %get-tuple-element.21.refs_0_.refs_2_, bf16[1,1024,1024]{2,1,0:T(8,128)(2,1)} %get-tuple-element.22.refs_1_.refs_3_, bf16[1,1024,1024]{2,1,0:T(8,128)(2,1)} %get-tuple-element.21.refs_0_.refs_2_, ...), custom_call_target="tpu_custom_call" | custom-call | flops 1 | bytes 1 | tf_op jit(solution)/shard_map/grads/pallas_call | solution.py:280
  162.0 67.1 %all-to-all-done.3.refs_0_.refs_1_ = f32[32,1,2,32,512]{4,3,2,1,0:T(8,128)} async-done(((f32[32,1,2,32,512]{4,3,2,1,0:T(8,128)}), f32[32,1,2,32,512]{4,3,2,1,0:T(8,128)}, u32[]{:S(2)}, u32[]{:S(2)}) %all-to-all-start.3) | async-done | bytes 4194336 | tf_op jit(solution)/shard_map/all_to_all | solution.py:335
  229.1 4.3 all-to-all-start.2
  233.4 11.3 %scaled.3 = (bf16[1,1024,1024]{2,1,0:T(8,128)(2,1)}, bf16[1,1024,1024]{2,1,0:T(8,128)(2,1)}, bf16[1,1024,512]{2,1,0:T(8,128)(2,1)}, bf16[1,1024,512]{2,1,0:T(8,1...) custom-call(s32[1]{0:T(128)} %bitcast.2.plane_ref, ...), custom_call_target="tpu_custom_call" | custom-call | flops 1 | bytes 1 | tf_op jit(solution)/shard_map/scaled/pallas_call | solution.py:243
  244.8 13.2 %grads.3 = f32[32,1,2,32,512]{4,3,2,1,0:T(8,128)} custom-call(s32[1]{0:T(128)} %bitcast.2.plane_ref, bf16[1,1024,1024]{2,1,0:T(8,128)(2,1)} %get-tuple-element.28.refs_0_.refs_2_, bf16[1,1024,1024]{2,1,0:T(8,128)(2,1)} %get-tuple-element.29.refs_1_.refs_3_, bf16[1,1024,1024]{2,1,0:T(8,128)(2,1)} %get-tuple-element.28.refs_0_.refs_2_, ...), custom_call_target="tpu_custom_call" | custom-call | flops 1 | bytes 1 | tf_op jit(solution)/shard_map/grads/pallas_call | solution.py:280
  258.0 69.2 %all-to-all-done.2.refs_4_ = f32[32,1,2,32,512]{4,3,2,1,0:T(8,128)} async-done(((f32[32,1,2,32,512]{4,3,2,1,0:T(8,128)}), f32[32,1,2,32,512]{4,3,2,1,0:T(8,128)}, u32[]{:S(2)}, u32[]{:S(2)}) %all-to-all-start.2) | async-done | bytes 4194336 | tf_op jit(solution)/shard_map/all_to_all | solution.py:335
  327.2 97.6 %all_to_all.29.refs_5_ = f32[32,1,2,32,512]{4,3,2,1,0:T(8,128)} all-to-all(f32[32,1,2,32,512]{4,3,2,1,0:T(8,128)} %grads.3), channel_id=1, replica_groups={{0,1,2,3,4,5,6,7,8,9,10,11,12,13,14,15,16,17,18,19,20,21,22,23,24,25,26..., dimensions={0} | all-to-all | bytes 8388608 | tf_op jit(solution)/shard_map/all_to_all | solution.py:335
  424.8 7.6 %place.1.grad_ref = f32[64,32,512]{2,1,0:T(8,128)} custom-call(s32[64]{0:T(128)} %reshape.63.refs_0_.refs_1_, s32[64]{0:T(128)} %reshape.63.refs_0_.refs_1_, s32[64]{0:T(128)} %reshape.64.refs_0_.refs_2_.refs_3_, s32[64]{0:T(128)} %reshape.64.refs_0_.refs_2_.refs_3_, f32[32,1,2,32,512]{4,3,2,1,0:T(8,128)} %all-to-all-done.2.refs_4_, ...), custom_call_target="tpu_custom_call" | custom-call | flops 1 | bytes 1 | tf_op jit(solution)/shard_map/place/pallas_call | solution.py:173
  432.4 5.2 %update.3 = (f32[32,32,512]{2,1,0:T(8,128)}, f32[32,32,512]{2,1,0:T(8,128)}) custom-call(f32[64,32,512]{2,1,0:T(8,128)} %place.1.grad_ref, f32[32,32,512]{2,1,0:T(8,128)} %table_ref.3, f32[32,32,512]{2,1,0:T(8,128)} %accum_ref.3), custom_call_target="tpu_custom_call" | custom-call | flops 1 | bytes 1 | tf_op jit(solution)/shard_map/update/pallas_call | solution.py:305
  437.7 5.2 %update.2 = (f32[32,32,512]{2,1,0:T(8,128)}, f32[32,32,512]{2,1,0:T(8,128)}) custom-call(f32[64,32,512]{2,1,0:T(8,128)} %place.1.grad_ref, f32[32,32,512]{2,1,0:T(8,128)} %table_ref.2, f32[32,32,512]{2,1,0:T(8,128)} %accum_ref.2), custom_call_target="tpu_custom_call" | custom-call | flops 1 | bytes 1 | tf_op jit(solution)/shard_map/update/pallas_call | solution.py:305
  (8 shorter events, 0.1 us)
Async XLA Ops:
  4.1 18.4 %all-to-all-start = ((f32[32,1,2176]{2,1,0:T(1,128)}), f32[32,1,2176]{2,1,0:T(1,128)S(1)}, u32[]{:S(2)}, u32[]{:S(2)}) async-start(f32[32,1,2176]{2,1,0:T(1,128)} %broadcast_in_dim.34), calls=%async_computation | async-start | bytes 557056 | tf_op jit(solution)/shard_map/all_to_all | solution.py:343
  28.5 97.6 %all-to-all-start.1 = ((f32[32,1,2,32,512]{4,3,2,1,0:T(8,128)}), f32[32,1,2,32,512]{4,3,2,1,0:T(8,128)}, u32[]{:S(2)}, u32[]{:S(2)}) async-start(f32[32,1,2,32,512]{4,3,2,1,0:T(8,128)} %pick.2), calls=%async_computation.1 | async-start | bytes 8388608 | tf_op jit(solution)/shard_map/all_to_all | solution.py:335
  131.3 97.8 %all-to-all-start.3 = ((f32[32,1,2,32,512]{4,3,2,1,0:T(8,128)}), f32[32,1,2,32,512]{4,3,2,1,0:T(8,128)}, u32[]{:S(2)}, u32[]{:S(2)}) async-start(f32[32,1,2,32,512]{4,3,2,1,0:T(8,128)} %pick.3), calls=%async_computation.3 | async-start | bytes 8388608 | tf_op jit(solution)/shard_map/all_to_all | solution.py:335
  229.1 98.1 %all-to-all-start.2 = ((f32[32,1,2,32,512]{4,3,2,1,0:T(8,128)}), f32[32,1,2,32,512]{4,3,2,1,0:T(8,128)}, u32[]{:S(2)}, u32[]{:S(2)}) async-start(f32[32,1,2,32,512]{4,3,2,1,0:T(8,128)} %grads.2), calls=%async_computation.2 | async-start | bytes 8388608 | tf_op jit(solution)/shard_map/all_to_all | solution.py:335

commit v2 on v0

v2 whole, which is shorter than its diff:
```python
import functools

import jax
import jax.numpy as jnp
from jax import lax
from jax.experimental import pallas as pl
from jax.experimental.pallas import tpu as pltpu
from jax.sharding import PartitionSpec as P

LANES = 128
VMEM_LIMIT = 56 * 1024 * 1024
F32 = jnp.float32
BF16 = jnp.bfloat16
COST = pl.CostEstimate(flops=1, bytes_accessed=1, transcendentals=0)


def params():
    return pltpu.CompilerParams(vmem_limit_bytes=VMEM_LIMIT)


def split(x):
    hi = x.astype(BF16)
    return hi, (x - hi.astype(F32)).astype(BF16)


def dot3(a_hi, a_lo, b_hi, b_lo, dims):
    def dot(a, b):
        return lax.dot_general(a, b, (dims, ((), ())), preferred_element_type=F32)

    return dot(a_hi, b_hi) + dot(a_hi, b_lo) + dot(a_lo, b_hi)


def block_major_kernel(row_ref, col_ref, out_ref):
    tiles = pl.num_programs(0) // 2

    @pl.when(pl.program_id(0) < tiles)
    def _():
        out_ref[...] = jnp.swapaxes(row_ref[...], 0, 1)

    @pl.when(pl.program_id(0) >= tiles)
    def _():
        out_ref[...] = jnp.swapaxes(col_ref[...], 0, 1)


def block_major(row_table, col_table):
    pos, blocks, width = row_table.shape
    tiles = blocks // 8
    return pl.pallas_call(
        block_major_kernel,
        grid=(2 * tiles,),
        in_specs=[
            pl.BlockSpec((pos, 8, width), lambda i: (0, jnp.minimum(i, tiles - 1), 0)),
            pl.BlockSpec((pos, 8, width), lambda i: (0, jnp.maximum(i - tiles, 0), 0)),
        ],
        out_specs=pl.BlockSpec((8, pos, width), lambda i: (i, 0, 0)),
        out_shape=jax.ShapeDtypeStruct((2 * blocks, pos, width), F32),
        compiler_params=params(),
        cost_estimate=COST,
        name="block_major",
    )(row_table, col_table)


def pick_kernel(index_ref, src_ref, out_ref):
    def step(j, carry):
        for k in range(out_ref.shape[1]):
            out_ref[j, k] = src_ref[index_ref[j * out_ref.shape[1] + k]]
        return carry

    lax.fori_loop(0, out_ref.shape[0], step, 0)


def pick(blocks, index, count):
    entries = index.shape[0]
    shape = (entries // count, count) + blocks.shape[1:]
    return pl.pallas_call(
        pick_kernel,
        grid_spec=pltpu.PrefetchScalarGridSpec(
            num_scalar_prefetch=1,
            grid=(1,),
            in_specs=[pl.BlockSpec(blocks.shape, lambda i, *_: (0, 0, 0))],
            out_specs=pl.BlockSpec(shape, lambda i, *_: (0, 0, 0, 0)),
        ),
        out_shape=jax.ShapeDtypeStruct(shape, F32),
        compiler_params=params(),
        cost_estimate=COST,
        name="pick",
    )(index, blocks)


def scaled_kernel(got_row, got_col, counts_ref, u_ref, v_ref, s_hi, s_lo, r_hi, r_lo, c_hi, c_lo):
    step = pl.program_id(0)
    rows, size = s_hi.shape

    @pl.when(step == 0)
    def _():
        for src, hi_ref, lo_ref in ((got_row, r_hi, r_lo), (got_col, c_hi, c_lo)):
            hi, lo = split(src[...].reshape(hi_ref.shape))
            hi_ref[...] = hi
            lo_ref[...] = lo

    mine = pl.ds(pl.multiple_of(step * rows, rows), rows)
    logits = dot3(r_hi[mine, :], r_lo[mine, :], c_hi[...], c_lo[...], ((1,), (1,)))
    tile_counts = counts_ref[0]
    values = tile_counts.astype(F32)
    target = jnp.log(jnp.maximum(values, 1.0)) - u_ref[0] - v_ref[0]
    error = logits - target
    confidence = 0.1 + 0.25 * jnp.sqrt(values)
    scaled = jnp.where(tile_counts > 0, confidence * error, jax.nn.sigmoid(error)) * (1.0 / size)
    hi, lo = split(scaled)
    s_hi[...] = hi
    s_lo[...] = lo


def scaled_parts(got, counts, u, v, shard, steps):
    size = counts.shape[1]
    devices, _, pos, width = got.shape
    rows = size // steps
    tile = pl.BlockSpec((rows, size), lambda i: (i, 0))
    whole = pl.BlockSpec((size, width), lambda i: (0, 0))
    return pl.pallas_call(
        scaled_kernel,
        grid=(steps,),
        in_specs=[
            pl.BlockSpec((devices, 1, pos, width), lambda i: (0, 0, 0, 0)),
            pl.BlockSpec((devices, 1, pos, width), lambda i: (0, 1, 0, 0)),
            pl.BlockSpec((1, rows, size), lambda i: (shard, i, 0)),
            pl.BlockSpec((1, rows, 1), lambda i: (shard, i, 0)),
            pl.BlockSpec((1, 1, size), lambda i: (shard, 0, 0)),
        ],
        out_specs=[tile] * 2 + [whole] * 4,
        out_shape=[jax.ShapeDtypeStruct((size, size), BF16)] * 2 + [jax.ShapeDtypeStruct((size, width), BF16)] * 4,
        compiler_params=params(),
        cost_estimate=COST,
        name="scaled",
    )(got, got, counts, u, v)


def grads_kernel(sr_hi, sr_lo, sc_hi, sc_lo, r_hi, r_lo, c_hi, c_lo, out_ref):
    devices, _, pos, width = out_ref.shape
    row_grad = dot3(sr_hi[...], sr_lo[...], c_hi[...], c_lo[...], ((1,), (0,)))
    out_ref[:, 0] = row_grad.reshape(devices, pos, width)
    col_grad = dot3(sc_hi[...], sc_lo[...], r_hi[...], r_lo[...], ((0,), (0,)))
    out_ref[:, 1] = col_grad.reshape(devices, pos, width)


def grads(parts, pos, steps):
    s_hi, s_lo, r_hi, r_lo, c_hi, c_lo = parts
    size, width = r_hi.shape
    rows = size // steps
    held = rows // pos
    across = pl.BlockSpec((rows, size), lambda i: (i, 0))
    down = pl.BlockSpec((size, rows), lambda i: (0, i))
    whole = pl.BlockSpec((size, width), lambda i: (0, 0))
    return pl.pallas_call(
        grads_kernel,
        grid=(steps,),
        in_specs=[across, across, down, down] + [whole] * 4,
        out_specs=pl.BlockSpec((held, 2, pos, width), lambda i: (i, 0, 0, 0)),
        out_shape=jax.ShapeDtypeStruct((size // pos, 2, pos, width), F32),
        compiler_params=params(),
        cost_estimate=COST,
        name="grads",
    )(s_hi, s_lo, s_hi, s_lo, r_hi, r_lo, c_hi, c_lo)


def update_kernel(sources, *refs):
    index_refs, refs = refs[:sources], refs[sources:]
    source_refs = refs[:sources]
    row, row_acc, col, col_acc, new_row, new_col, new_row_acc, new_col_acc, grad_ref = refs[sources:]
    step, tiles = pl.program_id(0), pl.num_programs(0) // 2

    @pl.when(step == 0)
    def _():
        grad_ref[...] = jnp.zeros_like(grad_ref)
        for index_ref, source_ref in zip(index_refs, source_refs):
            count = source_ref.shape[1]

            def add(j, carry, index_ref=index_ref, source_ref=source_ref, count=count):
                for k in range(count):
                    grad_ref[index_ref[j * count + k]] += source_ref[j, k]
                return carry

            lax.fori_loop(0, source_ref.shape[0], add, 0)

    def move(table_ref, accum_ref, new_table_ref, new_accum_ref):
        grad = jnp.swapaxes(grad_ref[pl.ds(pl.multiple_of(step * 8, 8), 8)], 0, 1)
        accum = accum_ref[...] + grad * grad
        new_accum_ref[...] = accum
        new_table_ref[...] = table_ref[...] - grad / jnp.sqrt(accum)

    @pl.when(step < tiles)
    def _():
        move(row, row_acc, new_row, new_row_acc)

    @pl.when(step >= tiles)
    def _():
        move(col, col_acc, new_col, new_col_acc)


def update(indices, sources, row_table, col_table, row_accum, col_accum):
    pos, blocks, width = row_table.shape
    tiles = blocks // 8
    row = pl.BlockSpec((pos, 8, width), lambda i, *_: (0, jnp.minimum(i, tiles - 1), 0))
    col = pl.BlockSpec((pos, 8, width), lambda i, *_: (0, jnp.maximum(i - tiles, 0), 0))
    return pl.pallas_call(
        functools.partial(update_kernel, len(sources)),
        grid_spec=pltpu.PrefetchScalarGridSpec(
            num_scalar_prefetch=len(indices),
            grid=(2 * tiles,),
            in_specs=[pl.BlockSpec(x.shape, lambda i, *_: (0, 0, 0, 0)) for x in sources] + [row, row, col, col],
            out_specs=[row, col, row, col],
            scratch_shapes=[pltpu.VMEM((2 * blocks, pos, width), F32)],
        ),
        out_shape=[jax.ShapeDtypeStruct(row_table.shape, F32)] * 4,
        compiler_params=params(),
        cost_estimate=COST,
        name="update",
    )(*indices, *sources, row_table, row_accum, col_table, col_accum)


def body(
    row_table, col_table, row_accum, col_accum, row_margin, col_margin, row_blocks, col_blocks, slot_of, counts, *, devices
):
    shards, size, _ = counts.shape
    pos, blocks, width = row_table.shape
    slots = 2 * blocks
    steps = 4

    def swap(x):
        return lax.all_to_all(x, "dev", 0, 0, tiled=True)

    every = jnp.arange(blocks, dtype=jnp.int32)
    ids = jnp.stack([row_blocks, col_blocks], axis=1)
    named = jnp.sum(jnp.where(ids[:, :, None] == every, slot_of, 0), axis=2) + jnp.array([0, blocks], jnp.int32)
    margins = jnp.concatenate([row_margin, col_margin], axis=1).reshape(-1)
    told = jnp.concatenate([jnp.pad(named.reshape(-1).astype(F32), (0, LANES - 2 * shards)), margins])
    told = swap(jnp.broadcast_to(told, (devices, told.shape[0])))
    tables = block_major(row_table, col_table)
    index = [told[:, 2 * shard : 2 * shard + 2].astype(jnp.int32).reshape(-1) for shard in range(shards)]

    sent, got = [], []
    for shard in range(shards):
        after = lax.optimization_barrier((index[shard], sent[-1]))[0] if sent else index[shard]
        sent.append(pick(tables, after, 2))
        got.append(swap(sent[-1]))

    margins = told[:, LANES:].reshape(size, slots)
    mine = named.reshape(2 * shards)
    margins = jnp.sum(jnp.where(mine[:, None, None] == jnp.arange(slots, dtype=jnp.int32), margins, 0.0), axis=2)
    margins = margins.reshape(shards, 2, size)
    u, v = margins[:, 0, :, None], margins[:, 1, None, :]

    back = []
    for shard in range(shards):
        parts = scaled_parts(got[shard], counts, u, v, shard, steps)
        back.append(swap(grads(parts, pos, steps)))
    return tuple(update(index, back, row_table, col_table, row_accum, col_accum))


def solution(mesh):
    spec = P("dev", None, None)
    flat = P("dev", None)
    return jax.shard_map(
        functools.partial(body, devices=mesh.shape["dev"]),
        mesh=mesh,
        in_specs=(spec, spec, spec, spec, flat, flat, P("dev"), P("dev"), P(), spec),
        out_specs=(spec, spec, spec, spec),
        check_vma=False,
    )
```

time: 554 us -> 435 us (0.79); the launches traced: 547 us -> 434 us
  waiting for transfers between devices: 320 us -> 233 us
  Pallas kernels: 0 us -> 76.9 us
  local copies, waits for them, and re-layouts: 77.2 us -> 4.82 us
  matrix products: 69.5 us -> 0 us
  blocking collectives: 42 us -> 97.7 us
  starting transfers between devices: 29.2 us -> 18.9 us
    all_to_all x0 -> x1, blocking collectives: none -> 97.7 us  [swap(): return lax.all_to_all(x, 'dev', 0, 0, tiled=True)]
    all_to_all x6 -> x4, waiting for transfers between devices: 320 us -> 233 us  [swap(): return lax.all_to_all(x, 'dev', 0, 0, tiled=True)]
    pallas_call x0 -> x8, Pallas kernels: none -> 76.9 us  [the longest x2 22.7 us: grads(): pl.pallas_call(grads_kernel, grid=(steps,), in_specs=[across, across, dow...]
    dot_general x8 -> x0, matrix products: 69.5 us -> none  [the longest x2 28.7 us: shard_grads(): jnp.dot(rows_block, cols_block.T, precision=high, preferred_element_type=...]
    unnamed x1 -> x0, blocking collectives: 42 us -> none
    all_to_all x10 -> x0, local copies, waits for them, and re-layouts: 33.4 us -> none  [the longest x2 12.7 us: body(): lax.all_to_all(out_rows, 'dev', split_axis=0, concat_axis=1, tiled=True)]
    gather x6 -> x0, local copies, waits for them, and re-layouts: 20.5 us -> none  [the longest x1 9.36 us: body(): send_cols = jnp.take(col_table, col_slots, axis=1)]
    all_to_all x6 -> x4, starting transfers between devices: 29.2 us -> 18.9 us  [swap(): return lax.all_to_all(x, 'dev', 0, 0, tiled=True)]
  transfers between devices with their start and end apart: 6 -> 4, of which waited for: 4 -> 4; matrix products, arithmetic and copies ran while one was open for 13% -> 1% of each run, Pallas kernels for 0% -> 13%
where the time goes in v2:
time: 435 us; the launch traced here: 434 us
  waiting for transfers between devices  233 us (54%)
  blocking collectives  97.7 us (22%)
  Pallas kernels  76.9 us (18%)
  starting transfers between devices  18.9 us (4%)
  local copies, waits for them, and re-layouts  4.82 us (1%)
    all_to_all x4, waiting for transfers between devices, swap(): return lax.all_to_all(x, 'dev', 0, 0, tiled=True)  233 us
    all_to_all x1, blocking collectives, swap(): return lax.all_to_all(x, 'dev', 0, 0, tiled=True)  97.7 us
    pallas_call x2, Pallas kernels, grads(): pl.pallas_call(grads_kernel, grid=(steps,), in_specs=[across, across, dow...  22.7 us
    pallas_call x2, Pallas kernels, scaled_parts(): pl.pallas_call(scaled_kernel, grid=(steps,), in_specs=[pl.BlockSpec((devi...  21.8 us
    all_to_all x4, starting transfers between devices, swap(): return lax.all_to_all(x, 'dev', 0, 0, tiled=True)  18.9 us
    pallas_call x1, Pallas kernels, update(): pl.pallas_call(functools.partial(update_kernel, len(sources)), grid_spec=...  14.7 us
    pallas_call x2, Pallas kernels, pick(): pl.pallas_call(pick_kernel, grid_spec=pltpu.PrefetchScalarGridSpec(num_sc...  10.5 us
  transfers between devices with their start and end apart: 4, of which 4 were waited for; matrix products, arithmetic and copies ran while one was open for 1% of the time, Pallas kernels for 13%

profile of v2, /device:TPU:0, one launch (start us, length us, event | category | flops | bytes accessed | tf_op | source)
XLA Modules:
  0.0 434.3 jit_solution(10310954063139948727)
XLA Ops:
  0.6 0.7 pad_add_fusion
  1.3 0.1 copy.24
  1.4 0.9 fusion
  2.3 0.1 add.20
  2.4 0.8 pad_maximum_fusion
  3.2 0.1 reshape.66
  3.3 0.9 broadcast_in_dim.33
  4.1 7.3 %all-to-all-start = ((f32[32,1,2176]{2,1,0:T(1,128)}), f32[32,1,2176]{2,1,0:T(1,128)S(1)}, u32[]{:S(2)}, u32[]{:S(2)}) async-start(f32[32,1,2176]{2,1,0:T(1,128)} %broadcast_in_dim.33), calls=%async_computation | async-start | bytes 557056 | tf_op jit(solution)/shard_map/all_to_all | solution.py:230
  11.4 7.2 %block_major.1.src_ref = f32[64,32,512]{2,1,0:T(8,128)} custom-call(f32[32,32,512]{2,1,0:T(8,128)} %refs_4_.1, f32[32,32,512]{2,1,0:T(8,128)} %refs_6_.1), custom_call_target="tpu_custom_call" | custom-call | flops 1 | bytes 1 | tf_op jit(solution)/shard_map/block_major/pallas_call | solution.py:48
  18.6 3.9 all-to-all-done
  22.6 0.1 slice_convert_fusion
  22.6 0.6 reshape.67.index_ref.refs_0_
  23.3 5.2 %pick.2 = f32[32,2,32,512]{3,2,1,0:T(8,128)} custom-call(s32[64]{0:T(128)} %reshape.67.index_ref.refs_0_, f32[64,32,512]{2,1,0:T(8,128)} %block_major.1.src_ref), custom_call_target="tpu_custom_call" | custom-call | flops 1 | bytes 1 | tf_op jit(solution)/shard_map/pick/pallas_call | solution.py:75
  28.5 3.6 all-to-all-start.1
  32.1 0.7 reshape.68.index_ref.refs_1_
  32.8 5.2 %pick.3 = f32[32,2,32,512]{3,2,1,0:T(8,128)} custom-call(s32[64]{0:T(128)} %reshape.68.index_ref.refs_1_, f32[64,32,512]{2,1,0:T(8,128)} %block_major.1.src_ref), custom_call_target="tpu_custom_call" | custom-call | flops 1 | bytes 1 | tf_op jit(solution)/shard_map/pick/pallas_call | solution.py:75
  38.0 88.1 %all-to-all-done.1.got_row.got_col = f32[32,2,32,512]{3,2,1,0:T(8,128)} async-done(((f32[32,2,32,512]{3,2,1,0:T(8,128)}), f32[32,2,32,512]{3,2,1,0:T(8,128)}, u32[]{:S(2)}, u32[]{:S(2)}) %all-to-all-start.1) | async-done | bytes 4194336 | tf_op jit(solution)/shard_map/all_to_all | solution.py:230
  126.1 3.9 all-to-all-start.3
  130.0 0.1 iota_compare_fusion.1
  130.1 0.2 reshape.69
  130.3 0.2 copy.25
  130.5 0.2 select_reduce_fusion
  130.7 0.6 fusion.1
  131.3 1.3 copy.26.u_ref
  132.7 10.9 %scaled.2 = (bf16[1024,1024]{1,0:T(8,128)(2,1)}, bf16[1024,1024]{1,0:T(8,128)(2,1)}, bf16[1024,512]{1,0:T(8,128)(2,1)}, bf16[1024,512]{1,0:T(8,128)(2,1)}, bf16[...) custom-call(f32[32,2,32,512]{3,2,1,0:T(8,128)} %all-to-all-done.1.got_row.got_col, ...), custom_call_target="tpu_custom_call" | custom-call | flops 1 | bytes 1 | tf_op jit(solution)/shard_map/scaled/pallas_call | solution.py:120
  143.5 11.3 %grads.2 = f32[32,2,32,512]{3,2,1,0:T(8,128)} custom-call(bf16[1024,1024]{1,0:T(8,128)(2,1)} %get-tuple-element.17.sr_hi.sc_hi, bf16[1024,1024]{1,0:T(8,128)(2,1)} %get-tuple-element.18.sr_lo.sc_lo, bf16[1024,1024]{1,0:T(8,128)(2,1)} %get-tuple-element.17.sr_hi.sc_hi, bf16[1024,1024]{1,0:T(8,128)(2,1)} %get-tuple-element.18.sr_lo.sc_lo, ...), custom_call_target="tpu_custom_call" | custom-call | flops 1 | bytes 1 | tf_op jit(solution)/shard_map/grads/pallas_call | solution.py:154
  154.9 69.0 %all-to-all-done.3.got_row.got_col = f32[32,2,32,512]{3,2,1,0:T(8,128)} async-done(((f32[32,2,32,512]{3,2,1,0:T(8,128)}), f32[32,2,32,512]{3,2,1,0:T(8,128)}, u32[]{:S(2)}, u32[]{:S(2)}) %all-to-all-start.3) | async-done | bytes 4194336 | tf_op jit(solution)/shard_map/all_to_all | solution.py:230
  223.9 4.1 all-to-all-start.2
  228.0 10.9 %scaled.3 = (bf16[1024,1024]{1,0:T(8,128)(2,1)}, bf16[1024,1024]{1,0:T(8,128)(2,1)}, bf16[1024,512]{1,0:T(8,128)(2,1)}, bf16[1024,512]{1,0:T(8,128)(2,1)}, bf16[...) custom-call(f32[32,2,32,512]{3,2,1,0:T(8,128)} %all-to-all-done.3.got_row.got_col, ...), custom_call_target="tpu_custom_call" | custom-call | flops 1 | bytes 1 | tf_op jit(solution)/shard_map/scaled/pallas_call | solution.py:120
  238.9 11.3 %grads.3 = f32[32,2,32,512]{3,2,1,0:T(8,128)} custom-call(bf16[1024,1024]{1,0:T(8,128)(2,1)} %get-tuple-element.24.sr_hi.sc_hi, bf16[1024,1024]{1,0:T(8,128)(2,1)} %get-tuple-element.25.sr_lo.sc_lo, bf16[1024,1024]{1,0:T(8,128)(2,1)} %get-tuple-element.24.sr_hi.sc_hi, bf16[1024,1024]{1,0:T(8,128)(2,1)} %get-tuple-element.25.sr_lo.sc_lo, ...), custom_call_target="tpu_custom_call" | custom-call | flops 1 | bytes 1 | tf_op jit(solution)/shard_map/grads/pallas_call | solution.py:154
  250.2 71.6 %all-to-all-done.2.refs_2_ = f32[32,2,32,512]{3,2,1,0:T(8,128)} async-done(((f32[32,2,32,512]{3,2,1,0:T(8,128)}), f32[32,2,32,512]{3,2,1,0:T(8,128)}, u32[]{:S(2)}, u32[]{:S(2)}) %all-to-all-start.2) | async-done | bytes 4194336 | tf_op jit(solution)/shard_map/all_to_all | solution.py:230
  321.8 97.7 %all_to_all.29.refs_3_ = f32[32,2,32,512]{3,2,1,0:T(8,128)} all-to-all(f32[32,2,32,512]{3,2,1,0:T(8,128)} %grads.3), channel_id=1, replica_groups=mesh['dev'=32] {'dev'}, dimensions={0} | all-to-all | bytes 8388608 | tf_op jit(solution)/shard_map/all_to_all | solution.py:230
  419.6 14.7 %update.1 = (f32[32,32,512]{2,1,0:T(8,128)}, f32[32,32,512]{2,1,0:T(8,128)}, f32[32,32,512]{2,1,0:T(8,128)}, f32[32,32,512]{2,1,0:T(8,128)}) custom-call(s32[64]{0:T(128)} %reshape.67.index_ref.refs_0_, s32[64]{0:T(128)} %reshape.68.index_ref.refs_1_, f32[32,2,32,512]{3,2,1,0:T(8,128)} %all-to-all-done.2.refs_2_, f32[32,2,32,512]{3,2,1,0:T(8,128)} %all_to_all.29.refs_3_, ...), custom_call_target="tpu_custom_call" | custom-call | flops 1 | bytes 1 | tf_op jit(solution)/shard_map/update/pallas_call | solution.py:205
  (7 shorter events, 0.1 us)
Async XLA Ops:
  4.1 18.4 %all-to-all-start = ((f32[32,1,2176]{2,1,0:T(1,128)}), f32[32,1,2176]{2,1,0:T(1,128)S(1)}, u32[]{:S(2)}, u32[]{:S(2)}) async-start(f32[32,1,2176]{2,1,0:T(1,128)} %broadcast_in_dim.33), calls=%async_computation | async-start | bytes 557056 | tf_op jit(solution)/shard_map/all_to_all | solution.py:230
  28.5 97.6 %all-to-all-start.1 = ((f32[32,2,32,512]{3,2,1,0:T(8,128)}), f32[32,2,32,512]{3,2,1,0:T(8,128)}, u32[]{:S(2)}, u32[]{:S(2)}) async-start(f32[32,2,32,512]{3,2,1,0:T(8,128)} %pick.2), calls=%async_computation.1 | async-start | bytes 8388608 | tf_op jit(solution)/shard_map/all_to_all | solution.py:230
  126.1 97.8 %all-to-all-start.3 = ((f32[32,2,32,512]{3,2,1,0:T(8,128)}), f32[32,2,32,512]{3,2,1,0:T(8,128)}, u32[]{:S(2)}, u32[]{:S(2)}) async-start(f32[32,2,32,512]{3,2,1,0:T(8,128)} %pick.3), calls=%async_computation.3 | async-start | bytes 8388608 | tf_op jit(solution)/shard_map/all_to_all | solution.py:230
  223.9 98.0 %all-to-all-start.2 = ((f32[32,2,32,512]{3,2,1,0:T(8,128)}), f32[32,2,32,512]{3,2,1,0:T(8,128)}, u32[]{:S(2)}, u32[]{:S(2)}) async-start(f32[32,2,32,512]{3,2,1,0:T(8,128)} %grads.2), calls=%async_computation.2 | async-start | bytes 8388608 | tf_op jit(solution)/shard_map/all_to_all | solution.py:230

commit v3 on v2

--- a/solution.py
+++ b/solution.py
@@ -60,20 +60,19 @@
     )(row_table, col_table)
 
 
-def pick_kernel(index_ref, src_ref, out_ref):
+def pick_kernel(shard, named_ref, src_ref, out_ref):
     def step(j, carry):
-        for k in range(out_ref.shape[1]):
-            out_ref[j, k] = src_ref[index_ref[j * out_ref.shape[1] + k]]
+        for k in range(2):
+            out_ref[j, k] = src_ref[named_ref[j, 2 * shard + k]]
         return carry
 
     lax.fori_loop(0, out_ref.shape[0], step, 0)
 
 
-def pick(blocks, index, count):
-    entries = index.shape[0]
-    shape = (entries // count, count) + blocks.shape[1:]
-    return pl.pallas_call(
-        pick_kernel,
+def pick(blocks, named, shard):
+    shape = (named.shape[0], 2) + blocks.shape[1:]
+    return pl.pallas_call(
+        functools.partial(pick_kernel, shard),
         grid_spec=pltpu.PrefetchScalarGridSpec(
             num_scalar_prefetch=1,
             grid=(1,),
@@ -84,7 +83,7 @@
         compiler_params=params(),
         cost_estimate=COST,
         name="pick",
-    )(index, blocks)
+    )(named, blocks)
 
 
 def scaled_kernel(got_row, got_col, counts_ref, u_ref, v_ref, s_hi, s_lo, r_hi, r_lo, c_hi, c_lo):
@@ -163,30 +162,50 @@
     )(s_hi, s_lo, s_hi, s_lo, r_hi, r_lo, c_hi, c_lo)
 
 
-def update_kernel(sources, *refs):
-    index_refs, refs = refs[:sources], refs[sources:]
-    source_refs = refs[:sources]
-    row, row_acc, col, col_acc, new_row, new_col, new_row_acc, new_col_acc, grad_ref = refs[sources:]
+def add_blocks(shard, named_ref, src_ref, grad_ref):
+    def add(j, carry):
+        for k in range(2):
+            grad_ref[named_ref[j, 2 * shard + k]] += src_ref[j, k]
+        return carry
+
+    grad_ref[...] = jnp.zeros_like(grad_ref)
+    lax.fori_loop(0, src_ref.shape[0], add, 0)
+
+
+def place(named, source, shard, slots):
+    shape = (slots,) + source.shape[2:]
+    return pl.pallas_call(
+        functools.partial(add_blocks, shard),
+        grid_spec=pltpu.PrefetchScalarGridSpec(
+            num_scalar_prefetch=1,
+            grid=(1,),
+            in_specs=[pl.BlockSpec(source.shape, lambda i, *_: (0, 0, 0, 0))],
+            out_specs=pl.BlockSpec(shape, lambda i, *_: (0, 0, 0)),
+        ),
+        out_shape=jax.ShapeDtypeStruct(shape, F32),
+        compiler_params=params(),
+        cost_estimate=COST,
+        name="place",
+    )(named, source)
+
+
+def update_kernel(shard, placed, named_ref, source_ref, *refs):
+    placed_refs, refs = refs[:placed], refs[placed:]
+    row, row_acc, col, col_acc, new_row, new_col, new_row_acc, new_col_acc, grad_ref = refs
     step, tiles = pl.program_id(0), pl.num_programs(0) // 2
 
     @pl.when(step == 0)
     def _():
-        grad_ref[...] = jnp.zeros_like(grad_ref)
-        for index_ref, source_ref in zip(index_refs, source_refs):
-            count = source_ref.shape[1]
-
-            def add(j, carry, index_ref=index_ref, source_ref=source_ref, count=count):
-                for k in range(count):
-                    grad_ref[index_ref[j * count + k]] += source_ref[j, k]
-                return carry
-
-            lax.fori_loop(0, source_ref.shape[0], add, 0)
+        add_blocks(shard, named_ref, source_ref, grad_ref)
 
     def move(table_ref, accum_ref, new_table_ref, new_accum_ref):
-        grad = jnp.swapaxes(grad_ref[pl.ds(pl.multiple_of(step * 8, 8), 8)], 0, 1)
+        grad = grad_ref[pl.ds(pl.multiple_of(step * 8, 8), 8)]
+        for placed_ref in placed_refs:
+            grad = grad + placed_ref[...]
+        grad = jnp.swapaxes(grad, 0, 1)
         accum = accum_ref[...] + grad * grad
         new_accum_ref[...] = accum
-        new_table_ref[...] = table_ref[...] - grad / jnp.sqrt(accum)
+        new_table_ref[...] = table_ref[...] - grad * lax.rsqrt(accum)
 
     @pl.when(step < tiles)
     def _():
@@ -197,17 +216,19 @@
         move(col, col_acc, new_col, new_col_acc)
 
 
-def update(indices, sources, row_table, col_table, row_accum, col_accum):
+def update(named, source, shard, placed, row_table, col_table, row_accum, col_accum):
     pos, blocks, width = row_table.shape
     tiles = blocks // 8
     row = pl.BlockSpec((pos, 8, width), lambda i, *_: (0, jnp.minimum(i, tiles - 1), 0))
     col = pl.BlockSpec((pos, 8, width), lambda i, *_: (0, jnp.maximum(i - tiles, 0), 0))
     return pl.pallas_call(
-        functools.partial(update_kernel, len(sources)),
+        functools.partial(update_kernel, shard, len(placed)),
         grid_spec=pltpu.PrefetchScalarGridSpec(
-            num_scalar_prefetch=len(indices),
+            num_scalar_prefetch=1,
             grid=(2 * tiles,),
-            in_specs=[pl.BlockSpec(x.shape, lambda i, *_: (0, 0, 0, 0)) for x in sources] + [row, row, col, col],
+            in_specs=[pl.BlockSpec(source.shape, lambda i, *_: (0, 0, 0, 0))]
+            + [pl.BlockSpec((8, pos, width), lambda i, *_: (i, 0, 0))] * len(placed)
+            + [row, row, col, col],
             out_specs=[row, col, row, col],
             scratch_shapes=[pltpu.VMEM((2 * blocks, pos, width), F32)],
         ),
@@ -215,7 +236,7 @@
         compiler_params=params(),
         cost_estimate=COST,
         name="update",
-    )(*indices, *sources, row_table, row_accum, col_table, col_accum)
+    )(named, source, *placed, row_table, row_accum, col_table, col_accum)
 
 
 def body(
@@ -231,21 +252,21 @@
 
     every = jnp.arange(blocks, dtype=jnp.int32)
     ids = jnp.stack([row_blocks, col_blocks], axis=1)
-    named = jnp.sum(jnp.where(ids[:, :, None] == every, slot_of, 0), axis=2) + jnp.array([0, blocks], jnp.int32)
+    mine = jnp.sum(jnp.where(ids[:, :, None] == every, slot_of, 0), axis=2) + jnp.array([0, blocks], jnp.int32)
+    mine = mine.reshape(2 * shards)
     margins = jnp.concatenate([row_margin, col_margin], axis=1).reshape(-1)
-    told = jnp.concatenate([jnp.pad(named.reshape(-1).astype(F32), (0, LANES - 2 * shards)), margins])
+    told = jnp.concatenate([jnp.pad(mine.astype(F32), (0, LANES - 2 * shards)), margins])
     told = swap(jnp.broadcast_to(told, (devices, told.shape[0])))
     tables = block_major(row_table, col_table)
-    index = [told[:, 2 * shard : 2 * shard + 2].astype(jnp.int32).reshape(-1) for shard in range(shards)]
+    named = told[:, :LANES].astype(jnp.int32)
 
     sent, got = [], []
     for shard in range(shards):
-        after = lax.optimization_barrier((index[shard], sent[-1]))[0] if sent else index[shard]
-        sent.append(pick(tables, after, 2))
+        after = lax.optimization_barrier((named, sent[-1]))[0] if sent else named
+        sent.append(pick(tables, after, shard))
         got.append(swap(sent[-1]))
 
     margins = told[:, LANES:].reshape(size, slots)
-    mine = named.reshape(2 * shards)
     margins = jnp.sum(jnp.where(mine[:, None, None] == jnp.arange(slots, dtype=jnp.int32), margins, 0.0), axis=2)
     margins = margins.reshape(shards, 2, size)
     u, v = margins[:, 0, :, None], margins[:, 1, None, :]
@@ -254,7 +275,8 @@
     for shard in range(shards):
         parts = scaled_parts(got[shard], counts, u, v, shard, steps)
         back.append(swap(grads(parts, pos, steps)))
-    return tuple(update(index, back, row_table, col_table, row_accum, col_accum))
+    placed = [place(named, back[shard], shard, slots) for shard in range(shards - 1)]
+    return tuple(update(named, back[-1], shards - 1, placed, row_table, col_table, row_accum, col_accum))
 
 
 def solution(mesh):

time: 435 us -> 435 us (level)
  blocking collectives: 97.7 us -> 0 us
  waiting for transfers between devices: 233 us -> 321 us
  Pallas kernels: 76.9 us -> 82.1 us
    all_to_all x1 -> x0, blocking collectives: 97.7 us -> none  [swap(): return lax.all_to_all(x, 'dev', 0, 0, tiled=True)]
    all_to_all x4 -> x5, waiting for transfers between devices: 233 us -> 321 us  [swap(): return lax.all_to_all(x, 'dev', 0, 0, tiled=True)]
    pallas_call x3 -> x4, Pallas kernels: 25.2 us -> 30.5 us  [the longest x1 13.6 us: update(): pl.pallas_call(functools.partial(update_kernel, shard, len(placed)), grid...]
    all_to_all x4 -> x5, starting transfers between devices: 18.9 us -> 23 us  [swap(): return lax.all_to_all(x, 'dev', 0, 0, tiled=True)]
  transfers between devices with their start and end apart: 4 -> 5, of which waited for: 4 -> 5; matrix products, arithmetic and copies ran while one was open for 1% -> 1% of each run, Pallas kernels for 13% -> 15%
where the time goes in v3:
time: 435 us; the launch traced here: 434 us
  waiting for transfers between devices  321 us (74%)
  Pallas kernels  82.1 us (19%)
  starting transfers between devices  23 us (5%)
    all_to_all x5, waiting for transfers between devices, swap(): return lax.all_to_all(x, 'dev', 0, 0, tiled=True)  321 us
    all_to_all x5, starting transfers between devices, swap(): return lax.all_to_all(x, 'dev', 0, 0, tiled=True)  23 us
    pallas_call x2, Pallas kernels, grads(): pl.pallas_call(grads_kernel, grid=(steps,), in_specs=[across, across, dow...  22.7 us
    pallas_call x2, Pallas kernels, scaled_parts(): pl.pallas_call(scaled_kernel, grid=(steps,), in_specs=[pl.BlockSpec((devi...  21.8 us
    pallas_call x1, Pallas kernels, update(): pl.pallas_call(functools.partial(update_kernel, shard, len(placed)), grid...  13.6 us
    pallas_call x2, Pallas kernels, pick(): pl.pallas_call(functools.partial(pick_kernel, shard), grid_spec=pltpu.Pre...  11 us
  transfers between devices with their start and end apart: 5, of which 5 were waited for; matrix products, arithmetic and copies ran while one was open for 1% of the time, Pallas kernels for 15%

profile of v3, /device:TPU:0, one launch (start us, length us, event | category | flops | bytes accessed | tf_op | source)
XLA Modules:
  0.0 433.6 jit_solution(13193544448028906776)
XLA Ops:
  0.6 0.7 pad_add_fusion
  1.3 0.1 copy.24
  1.4 0.9 fusion
  2.3 0.1 add.20
  2.4 0.8 pad_maximum_fusion
  3.2 0.1 reshape.60
  3.3 0.9 broadcast_in_dim.33
  4.1 7.3 %all-to-all-start = ((f32[32,1,2176]{2,1,0:T(1,128)}), f32[32,1,2176]{2,1,0:T(1,128)S(1)}, u32[]{:S(2)}, u32[]{:S(2)}) async-start(f32[32,1,2176]{2,1,0:T(1,128)} %broadcast_in_dim.33), calls=%async_computation | async-start | bytes 557056 | tf_op jit(solution)/shard_map/all_to_all | solution.py:251
  11.4 7.1 %block_major.1.src_ref = f32[64,32,512]{2,1,0:T(8,128)} custom-call(f32[32,32,512]{2,1,0:T(8,128)} %refs_1_.1, f32[32,32,512]{2,1,0:T(8,128)} %refs_3_.1), custom_call_target="tpu_custom_call" | custom-call | flops 1 | bytes 1 | tf_op jit(solution)/shard_map/block_major/pallas_call | solution.py:48
  18.6 4.0 all-to-all-done
  22.6 0.6 slice_convert_fusion.named_ref
  23.2 5.5 %pick.2 = f32[32,2,32,512]{3,2,1,0:T(8,128)} custom-call(s32[32,128]{1,0:T(8,128)} %slice_convert_fusion.named_ref, f32[64,32,512]{2,1,0:T(8,128)} %block_major.1.src_ref), custom_call_target="tpu_custom_call" | custom-call | flops 1 | bytes 1 | tf_op jit(solution)/shard_map/pick/pallas_call | solution.py:74
  28.7 3.6 all-to-all-start.3
  32.2 5.5 %pick.3 = f32[32,2,32,512]{3,2,1,0:T(8,128)} custom-call(s32[32,128]{1,0:T(8,128)} %slice_convert_fusion.named_ref, f32[64,32,512]{2,1,0:T(8,128)} %block_major.1.src_ref), custom_call_target="tpu_custom_call" | custom-call | flops 1 | bytes 1 | tf_op jit(solution)/shard_map/pick/pallas_call | solution.py:74
  37.7 88.5 %all-to-all-done.3.got_row.got_col = f32[32,2,32,512]{3,2,1,0:T(8,128)} async-done(((f32[32,2,32,512]{3,2,1,0:T(8,128)}), f32[32,2,32,512]{3,2,1,0:T(8,128)}, u32[]{:S(2)}, u32[]{:S(2)}) %all-to-all-start.3) | async-done | bytes 4194336 | tf_op jit(solution)/shard_map/all_to_all | solution.py:251
  126.2 3.9 all-to-all-start.1
  130.2 0.1 iota_compare_fusion.1
  130.2 0.2 reshape.61
  130.5 0.2 copy.25
  130.7 0.2 select_reduce_fusion
  130.9 0.6 fusion.1
  131.5 1.3 copy.26.u_ref
  132.8 10.9 %scaled.3 = (bf16[1024,1024]{1,0:T(8,128)(2,1)}, bf16[1024,1024]{1,0:T(8,128)(2,1)}, bf16[1024,512]{1,0:T(8,128)(2,1)}, bf16[1024,512]{1,0:T(8,128)(2,1)}, bf16[...) custom-call(f32[32,2,32,512]{3,2,1,0:T(8,128)} %all-to-all-done.3.got_row.got_col, ...), custom_call_target="tpu_custom_call" | custom-call | flops 1 | bytes 1 | tf_op jit(solution)/shard_map/scaled/pallas_call | solution.py:119
  143.7 11.3 %grads.3 = f32[32,2,32,512]{3,2,1,0:T(8,128)} custom-call(bf16[1024,1024]{1,0:T(8,128)(2,1)} %get-tuple-element.24.sr_hi.sc_hi, bf16[1024,1024]{1,0:T(8,128)(2,1)} %get-tuple-element.25.sr_lo.sc_lo, bf16[1024,1024]{1,0:T(8,128)(2,1)} %get-tuple-element.24.sr_hi.sc_hi, bf16[1024,1024]{1,0:T(8,128)(2,1)} %get-tuple-element.25.sr_lo.sc_lo, ...), custom_call_target="tpu_custom_call" | custom-call | flops 1 | bytes 1 | tf_op jit(solution)/shard_map/grads/pallas_call | solution.py:153
  155.0 69.0 %all-to-all-done.1.got_row.got_col = f32[32,2,32,512]{3,2,1,0:T(8,128)} async-done(((f32[32,2,32,512]{3,2,1,0:T(8,128)}), f32[32,2,32,512]{3,2,1,0:T(8,128)}, u32[]{:S(2)}, u32[]{:S(2)}) %all-to-all-start.1) | async-done | bytes 4194336 | tf_op jit(solution)/shard_map/all_to_all | solution.py:251
  224.0 4.1 all-to-all-start.4
  228.1 10.9 %scaled.2 = (bf16[1024,1024]{1,0:T(8,128)(2,1)}, bf16[1024,1024]{1,0:T(8,128)(2,1)}, bf16[1024,512]{1,0:T(8,128)(2,1)}, bf16[1024,512]{1,0:T(8,128)(2,1)}, bf16[...) custom-call(f32[32,2,32,512]{3,2,1,0:T(8,128)} %all-to-all-done.1.got_row.got_col, ...), custom_call_target="tpu_custom_call" | custom-call | flops 1 | bytes 1 | tf_op jit(solution)/shard_map/scaled/pallas_call | solution.py:119
  239.0 11.3 %grads.2 = f32[32,2,32,512]{3,2,1,0:T(8,128)} custom-call(bf16[1024,1024]{1,0:T(8,128)(2,1)} %get-tuple-element.18.sr_hi.sc_hi, bf16[1024,1024]{1,0:T(8,128)(2,1)} %get-tuple-element.19.sr_lo.sc_lo, bf16[1024,1024]{1,0:T(8,128)(2,1)} %get-tuple-element.18.sr_hi.sc_hi, bf16[1024,1024]{1,0:T(8,128)(2,1)} %get-tuple-element.19.sr_lo.sc_lo, ...), custom_call_target="tpu_custom_call" | custom-call | flops 1 | bytes 1 | tf_op jit(solution)/shard_map/grads/pallas_call | solution.py:153
  250.4 71.6 %all-to-all-done.4.src_ref = f32[32,2,32,512]{3,2,1,0:T(8,128)} async-done(((f32[32,2,32,512]{3,2,1,0:T(8,128)}), f32[32,2,32,512]{3,2,1,0:T(8,128)}, u32[]{:S(2)}, u32[]{:S(2)}) %all-to-all-start.4) | async-done | bytes 4194336 | tf_op jit(solution)/shard_map/all_to_all | solution.py:251
  322.0 4.1 all-to-all-start.2
  326.1 5.9 %place.1.refs_0_ = f32[64,32,512]{2,1,0:T(8,128)} custom-call(s32[32,128]{1,0:T(8,128)} %slice_convert_fusion.named_ref, f32[32,2,32,512]{3,2,1,0:T(8,128)} %all-to-all-done.4.src_ref), custom_call_target="tpu_custom_call" | custom-call | flops 1 | bytes 1 | tf_op jit(solution)/shard_map/place/pallas_call | solution.py:177
  332.0 88.0 %all-to-all-done.2.source_ref = f32[32,2,32,512]{3,2,1,0:T(8,128)} async-done(((f32[32,2,32,512]{3,2,1,0:T(8,128)}), f32[32,2,32,512]{3,2,1,0:T(8,128)}, u32[]{:S(2)}, u32[]{:S(2)}) %all-to-all-start.2) | async-done | bytes 4194336 | tf_op jit(solution)/shard_map/all_to_all | solution.py:251
  420.0 13.6 %update.1 = (f32[32,32,512]{2,1,0:T(8,128)}, f32[32,32,512]{2,1,0:T(8,128)}, f32[32,32,512]{2,1,0:T(8,128)}, f32[32,32,512]{2,1,0:T(8,128)}) custom-call(s32[32,128]{1,0:T(8,128)} %slice_convert_fusion.named_ref, f32[32,2,32,512]{3,2,1,0:T(8,128)} %all-to-all-done.2.source_ref, f32[64,32,512]{2,1,0:T(8,128)} %place.1.refs_0_, f32[32,32,512]{2,1,0:T(8,128)} %refs_1_.1, ...), custom_call_target="tpu_custom_call" | custom-call | flops 1 | bytes 1 | tf_op jit(solution)/shard_map/update/pallas_call | solution.py:224
  (7 shorter events, 0.1 us)
Async XLA Ops:
  4.1 18.4 %all-to-all-start = ((f32[32,1,2176]{2,1,0:T(1,128)}), f32[32,1,2176]{2,1,0:T(1,128)S(1)}, u32[]{:S(2)}, u32[]{:S(2)}) async-start(f32[32,1,2176]{2,1,0:T(1,128)} %broadcast_in_dim.33), calls=%async_computation | async-start | bytes 557056 | tf_op jit(solution)/shard_map/all_to_all | solution.py:251
  28.7 97.6 %all-to-all-start.3 = ((f32[32,2,32,512]{3,2,1,0:T(8,128)}), f32[32,2,32,512]{3,2,1,0:T(8,128)}, u32[]{:S(2)}, u32[]{:S(2)}) async-start(f32[32,2,32,512]{3,2,1,0:T(8,128)} %pick.2), calls=%async_computation.3 | async-start | bytes 8388608 | tf_op jit(solution)/shard_map/all_to_all | solution.py:251
  126.2 97.8 %all-to-all-start.1 = ((f32[32,2,32,512]{3,2,1,0:T(8,128)}), f32[32,2,32,512]{3,2,1,0:T(8,128)}, u32[]{:S(2)}, u32[]{:S(2)}) async-start(f32[32,2,32,512]{3,2,1,0:T(8,128)} %pick.3), calls=%async_computation.1 | async-start | bytes 8388608 | tf_op jit(solution)/shard_map/all_to_all | solution.py:251
  224.0 98.0 %all-to-all-start.4 = ((f32[32,2,32,512]{3,2,1,0:T(8,128)}), f32[32,2,32,512]{3,2,1,0:T(8,128)}, u32[]{:S(2)}, u32[]{:S(2)}) async-start(f32[32,2,32,512]{3,2,1,0:T(8,128)} %grads.3), calls=%async_computation.4 | async-start | bytes 8388608 | tf_op jit(solution)/shard_map/all_to_all | solution.py:251
  322.0 98.0 %all-to-all-start.2 = ((f32[32,2,32,512]{3,2,1,0:T(8,128)}), f32[32,2,32,512]{3,2,1,0:T(8,128)}, u32[]{:S(2)}, u32[]{:S(2)}) async-start(f32[32,2,32,512]{3,2,1,0:T(8,128)} %grads.2), calls=%async_computation.2 | async-start | bytes 8388608 | tf_op jit(solution)/shard_map/all_to_all | solution.py:251

commit v4 on v3

--- a/solution.py
+++ b/solution.py
@@ -61,25 +61,28 @@
 
 
 def pick_kernel(shard, named_ref, src_ref, out_ref):
+    kind = pl.program_id(0)
+    first = kind * src_ref.shape[0]
+
     def step(j, carry):
-        for k in range(2):
-            out_ref[j, k] = src_ref[named_ref[j, 2 * shard + k]]
+        out_ref[j, 0] = src_ref[named_ref[j, 2 * shard + kind] - first]
         return carry
 
     lax.fori_loop(0, out_ref.shape[0], step, 0)
 
 
 def pick(blocks, named, shard):
-    shape = (named.shape[0], 2) + blocks.shape[1:]
+    slots, pos, width = blocks.shape
+    devices = named.shape[0]
     return pl.pallas_call(
         functools.partial(pick_kernel, shard),
         grid_spec=pltpu.PrefetchScalarGridSpec(
             num_scalar_prefetch=1,
-            grid=(1,),
-            in_specs=[pl.BlockSpec(blocks.shape, lambda i, *_: (0, 0, 0))],
-            out_specs=pl.BlockSpec(shape, lambda i, *_: (0, 0, 0, 0)),
+            grid=(2,),
+            in_specs=[pl.BlockSpec((slots // 2, pos, width), lambda i, *_: (i, 0, 0))],
+            out_specs=pl.BlockSpec((devices, 1, pos, width), lambda i, *_: (0, i, 0, 0)),
         ),
-        out_shape=jax.ShapeDtypeStruct(shape, F32),
+        out_shape=jax.ShapeDtypeStruct((devices, 2, pos, width), F32),
         compiler_params=params(),
         cost_estimate=COST,
         name="pick",
@@ -194,12 +197,22 @@
     row, row_acc, col, col_acc, new_row, new_col, new_row_acc, new_col_acc, grad_ref = refs
     step, tiles = pl.program_id(0), pl.num_programs(0) // 2
 
-    @pl.when(step == 0)
-    def _():
-        add_blocks(shard, named_ref, source_ref, grad_ref)
+    kind = step // tiles
+    inner = step - kind * tiles
+
+    @pl.when(inner == 0)
+    def _():
+        first = kind * grad_ref.shape[0]
+
+        def add(j, carry):
+            grad_ref[named_ref[j, 2 * shard + kind] - first] += source_ref[j, 0]
+            return carry
+
+        grad_ref[...] = jnp.zeros_like(grad_ref)
+        lax.fori_loop(0, source_ref.shape[0], add, 0)
 
     def move(table_ref, accum_ref, new_table_ref, new_accum_ref):
-        grad = grad_ref[pl.ds(pl.multiple_of(step * 8, 8), 8)]
+        grad = grad_ref[pl.ds(pl.multiple_of(inner * 8, 8), 8)]
         for placed_ref in placed_refs:
             grad = grad + placed_ref[...]
         grad = jnp.swapaxes(grad, 0, 1)
@@ -226,11 +239,11 @@
         grid_spec=pltpu.PrefetchScalarGridSpec(
             num_scalar_prefetch=1,
             grid=(2 * tiles,),
-            in_specs=[pl.BlockSpec(source.shape, lambda i, *_: (0, 0, 0, 0))]
+            in_specs=[pl.BlockSpec((source.shape[0], 1, pos, width), lambda i, *_: (0, i // tiles, 0, 0))]
             + [pl.BlockSpec((8, pos, width), lambda i, *_: (i, 0, 0))] * len(placed)
             + [row, row, col, col],
             out_specs=[row, col, row, col],
-            scratch_shapes=[pltpu.VMEM((2 * blocks, pos, width), F32)],
+            scratch_shapes=[pltpu.VMEM((blocks, pos, width), F32)],
         ),
         out_shape=[jax.ShapeDtypeStruct(row_table.shape, F32)] * 4,
         compiler_params=params(),

time: 435 us -> 434 us (level)
  transfers between devices with their start and end apart: 5 -> 5, of which waited for: 5 -> 5; matrix products, arithmetic and copies ran while one was open for 1% -> 1% of each run, Pallas kernels for 15% -> 14%
where the time goes in v4:
time: 434 us; the launch traced here: 433 us
  waiting for transfers between devices  322 us (74%)
  Pallas kernels  80.7 us (19%)
  starting transfers between devices  23 us (5%)
    all_to_all x5, waiting for transfers between devices, swap(): return lax.all_to_all(x, 'dev', 0, 0, tiled=True)  322 us
    all_to_all x5, starting transfers between devices, swap(): return lax.all_to_all(x, 'dev', 0, 0, tiled=True)  23 us
    pallas_call x2, Pallas kernels, grads(): pl.pallas_call(grads_kernel, grid=(steps,), in_specs=[across, across, dow...  22.7 us
    pallas_call x2, Pallas kernels, scaled_parts(): pl.pallas_call(scaled_kernel, grid=(steps,), in_specs=[pl.BlockSpec((devi...  21.8 us
    pallas_call x1, Pallas kernels, update(): pl.pallas_call(functools.partial(update_kernel, shard, len(placed)), grid...  13.6 us
    pallas_call x2, Pallas kernels, pick(): pl.pallas_call(functools.partial(pick_kernel, shard), grid_spec=pltpu.Pre...  9.67 us
  transfers between devices with their start and end apart: 5, of which 5 were waited for; matrix products, arithmetic and copies ran while one was open for 1% of the time, Pallas kernels for 14%

profile of v4, /device:TPU:0, one launch (start us, length us, event | category | flops | bytes accessed | tf_op | source)
XLA Modules:
  0.0 432.9 jit_solution(818114469574925531)
XLA Ops:
  0.6 0.7 pad_add_fusion
  1.3 0.1 copy.24
  1.4 0.9 fusion
  2.3 0.1 add.20
  2.4 0.8 pad_maximum_fusion
  3.2 0.1 reshape.60
  3.3 0.9 broadcast_in_dim.33
  4.1 7.3 %all-to-all-start = ((f32[32,1,2176]{2,1,0:T(1,128)}), f32[32,1,2176]{2,1,0:T(1,128)S(1)}, u32[]{:S(2)}, u32[]{:S(2)}) async-start(f32[32,1,2176]{2,1,0:T(1,128)} %broadcast_in_dim.33), calls=%async_computation | async-start | bytes 557056 | tf_op jit(solution)/shard_map/all_to_all | solution.py:264
  11.4 7.1 %block_major.1.src_ref = f32[64,32,512]{2,1,0:T(8,128)} custom-call(f32[32,32,512]{2,1,0:T(8,128)} %refs_1_.1, f32[32,32,512]{2,1,0:T(8,128)} %refs_3_.1), custom_call_target="tpu_custom_call" | custom-call | flops 1 | bytes 1 | tf_op jit(solution)/shard_map/block_major/pallas_call | solution.py:48
  18.6 4.0 all-to-all-done
  22.6 0.6 slice_convert_fusion.named_ref
  23.2 4.8 %pick.2 = f32[32,2,32,512]{3,2,1,0:T(8,128)} custom-call(s32[32,128]{1,0:T(8,128)} %slice_convert_fusion.named_ref, f32[64,32,512]{2,1,0:T(8,128)} %block_major.1.src_ref), custom_call_target="tpu_custom_call" | custom-call | flops 1 | bytes 1 | tf_op jit(solution)/shard_map/pick/pallas_call | solution.py:77
  28.0 3.6 all-to-all-start.3
  31.6 4.9 %pick.3 = f32[32,2,32,512]{3,2,1,0:T(8,128)} custom-call(s32[32,128]{1,0:T(8,128)} %slice_convert_fusion.named_ref, f32[64,32,512]{2,1,0:T(8,128)} %block_major.1.src_ref), custom_call_target="tpu_custom_call" | custom-call | flops 1 | bytes 1 | tf_op jit(solution)/shard_map/pick/pallas_call | solution.py:77
  36.4 89.2 %all-to-all-done.3.got_row.got_col = f32[32,2,32,512]{3,2,1,0:T(8,128)} async-done(((f32[32,2,32,512]{3,2,1,0:T(8,128)}), f32[32,2,32,512]{3,2,1,0:T(8,128)}, u32[]{:S(2)}, u32[]{:S(2)}) %all-to-all-start.3) | async-done | bytes 4194336 | tf_op jit(solution)/shard_map/all_to_all | solution.py:264
  125.6 3.9 all-to-all-start.1
  129.5 0.1 iota_compare_fusion.1
  129.6 0.2 reshape.61
  129.8 0.2 copy.25
  130.0 0.2 select_reduce_fusion
  130.2 0.6 fusion.1
  130.8 1.3 copy.26.u_ref
  132.1 10.9 %scaled.3 = (bf16[1024,1024]{1,0:T(8,128)(2,1)}, bf16[1024,1024]{1,0:T(8,128)(2,1)}, bf16[1024,512]{1,0:T(8,128)(2,1)}, bf16[1024,512]{1,0:T(8,128)(2,1)}, bf16[...) custom-call(f32[32,2,32,512]{3,2,1,0:T(8,128)} %all-to-all-done.3.got_row.got_col, ...), custom_call_target="tpu_custom_call" | custom-call | flops 1 | bytes 1 | tf_op jit(solution)/shard_map/scaled/pallas_call | solution.py:122
  143.0 11.3 %grads.3 = f32[32,2,32,512]{3,2,1,0:T(8,128)} custom-call(bf16[1024,1024]{1,0:T(8,128)(2,1)} %get-tuple-element.24.sr_hi.sc_hi, bf16[1024,1024]{1,0:T(8,128)(2,1)} %get-tuple-element.25.sr_lo.sc_lo, bf16[1024,1024]{1,0:T(8,128)(2,1)} %get-tuple-element.24.sr_hi.sc_hi, bf16[1024,1024]{1,0:T(8,128)(2,1)} %get-tuple-element.25.sr_lo.sc_lo, ...), custom_call_target="tpu_custom_call" | custom-call | flops 1 | bytes 1 | tf_op jit(solution)/shard_map/grads/pallas_call | solution.py:156
  154.4 69.0 %all-to-all-done.1.got_row.got_col = f32[32,2,32,512]{3,2,1,0:T(8,128)} async-done(((f32[32,2,32,512]{3,2,1,0:T(8,128)}), f32[32,2,32,512]{3,2,1,0:T(8,128)}, u32[]{:S(2)}, u32[]{:S(2)}) %all-to-all-start.1) | async-done | bytes 4194336 | tf_op jit(solution)/shard_map/all_to_all | solution.py:264
  223.4 4.1 all-to-all-start.4
  227.5 10.9 %scaled.2 = (bf16[1024,1024]{1,0:T(8,128)(2,1)}, bf16[1024,1024]{1,0:T(8,128)(2,1)}, bf16[1024,512]{1,0:T(8,128)(2,1)}, bf16[1024,512]{1,0:T(8,128)(2,1)}, bf16[...) custom-call(f32[32,2,32,512]{3,2,1,0:T(8,128)} %all-to-all-done.1.got_row.got_col, ...), custom_call_target="tpu_custom_call" | custom-call | flops 1 | bytes 1 | tf_op jit(solution)/shard_map/scaled/pallas_call | solution.py:122
  238.4 11.3 %grads.2 = f32[32,2,32,512]{3,2,1,0:T(8,128)} custom-call(bf16[1024,1024]{1,0:T(8,128)(2,1)} %get-tuple-element.18.sr_hi.sc_hi, bf16[1024,1024]{1,0:T(8,128)(2,1)} %get-tuple-element.19.sr_lo.sc_lo, bf16[1024,1024]{1,0:T(8,128)(2,1)} %get-tuple-element.18.sr_hi.sc_hi, bf16[1024,1024]{1,0:T(8,128)(2,1)} %get-tuple-element.19.sr_lo.sc_lo, ...), custom_call_target="tpu_custom_call" | custom-call | flops 1 | bytes 1 | tf_op jit(solution)/shard_map/grads/pallas_call | solution.py:156
  249.7 71.6 %all-to-all-done.4.src_ref = f32[32,2,32,512]{3,2,1,0:T(8,128)} async-done(((f32[32,2,32,512]{3,2,1,0:T(8,128)}), f32[32,2,32,512]{3,2,1,0:T(8,128)}, u32[]{:S(2)}, u32[]{:S(2)}) %all-to-all-start.4) | async-done | bytes 4194336 | tf_op jit(solution)/shard_map/all_to_all | solution.py:264
  321.3 4.1 all-to-all-start.2
  325.4 5.9 %place.1.refs_0_ = f32[64,32,512]{2,1,0:T(8,128)} custom-call(s32[32,128]{1,0:T(8,128)} %slice_convert_fusion.named_ref, f32[32,2,32,512]{3,2,1,0:T(8,128)} %all-to-all-done.4.src_ref), custom_call_target="tpu_custom_call" | custom-call | flops 1 | bytes 1 | tf_op jit(solution)/shard_map/place/pallas_call | solution.py:180
  331.3 88.0 %all-to-all-done.2.source_ref = f32[32,2,32,512]{3,2,1,0:T(8,128)} async-done(((f32[32,2,32,512]{3,2,1,0:T(8,128)}), f32[32,2,32,512]{3,2,1,0:T(8,128)}, u32[]{:S(2)}, u32[]{:S(2)}) %all-to-all-start.2) | async-done | bytes 4194336 | tf_op jit(solution)/shard_map/all_to_all | solution.py:264
  419.3 13.6 %update.1 = (f32[32,32,512]{2,1,0:T(8,128)}, f32[32,32,512]{2,1,0:T(8,128)}, f32[32,32,512]{2,1,0:T(8,128)}, f32[32,32,512]{2,1,0:T(8,128)}) custom-call(s32[32,128]{1,0:T(8,128)} %slice_convert_fusion.named_ref, f32[32,2,32,512]{3,2,1,0:T(8,128)} %all-to-all-done.2.source_ref, f32[64,32,512]{2,1,0:T(8,128)} %place.1.refs_0_, f32[32,32,512]{2,1,0:T(8,128)} %refs_1_.1, ...), custom_call_target="tpu_custom_call" | custom-call | flops 1 | bytes 1 | tf_op jit(solution)/shard_map/update/pallas_call | solution.py:237
  (7 shorter events, 0.1 us)
Async XLA Ops:
  4.1 18.4 %all-to-all-start = ((f32[32,1,2176]{2,1,0:T(1,128)}), f32[32,1,2176]{2,1,0:T(1,128)S(1)}, u32[]{:S(2)}, u32[]{:S(2)}) async-start(f32[32,1,2176]{2,1,0:T(1,128)} %broadcast_in_dim.33), calls=%async_computation | async-start | bytes 557056 | tf_op jit(solution)/shard_map/all_to_all | solution.py:264
  28.0 97.6 %all-to-all-start.3 = ((f32[32,2,32,512]{3,2,1,0:T(8,128)}), f32[32,2,32,512]{3,2,1,0:T(8,128)}, u32[]{:S(2)}, u32[]{:S(2)}) async-start(f32[32,2,32,512]{3,2,1,0:T(8,128)} %pick.2), calls=%async_computation.3 | async-start | bytes 8388608 | tf_op jit(solution)/shard_map/all_to_all | solution.py:264
  125.6 97.8 %all-to-all-start.1 = ((f32[32,2,32,512]{3,2,1,0:T(8,128)}), f32[32,2,32,512]{3,2,1,0:T(8,128)}, u32[]{:S(2)}, u32[]{:S(2)}) async-start(f32[32,2,32,512]{3,2,1,0:T(8,128)} %pick.3), calls=%async_computation.1 | async-start | bytes 8388608 | tf_op jit(solution)/shard_map/all_to_all | solution.py:264
  223.4 98.0 %all-to-all-start.4 = ((f32[32,2,32,512]{3,2,1,0:T(8,128)}), f32[32,2,32,512]{3,2,1,0:T(8,128)}, u32[]{:S(2)}, u32[]{:S(2)}) async-start(f32[32,2,32,512]{3,2,1,0:T(8,128)} %grads.3), calls=%async_computation.4 | async-start | bytes 8388608 | tf_op jit(solution)/shard_map/all_to_all | solution.py:264
  321.3 98.0 %all-to-all-start.2 = ((f32[32,2,32,512]{3,2,1,0:T(8,128)}), f32[32,2,32,512]{3,2,1,0:T(8,128)}, u32[]{:S(2)}, u32[]{:S(2)}) async-start(f32[32,2,32,512]{3,2,1,0:T(8,128)} %grads.2), calls=%async_computation.2 | async-start | bytes 8388608 | tf_op jit(solution)/shard_map/all_to_all | solution.py:264
